TPU v7x, 128 devices: a whole 4x4x4 slice. The times are simulated.
128 devices in a mesh: wide: 32 (over y, z, core), narrow: 4 (over x).
Axes of the slice: x: 4, y: 4, z: 4, core: 2. Of those that a mesh axis runs over, the one named last changes fastest.
Arguments:
- coefficients: float32 [16, 256, 32, 128], P('narrow', 'wide'), may hold values from -6 to 6
- observed: float32 [16, 256, 32, 128], P('narrow', 'wide'), may hold values from -6 to 6
- blocks: bfloat16 [4, 32, 128, 128, 128], P('narrow', 'wide'), may hold values from -0.3125 to 0.3125
- block_rows: int32 [4, 32, 128], P('narrow', 'wide'), may hold values from 0 to 31
- block_cols: int32 [4, 32, 128], P('narrow', 'wide'), may hold values from 0 to 59, as said below
- live_count: int32 [4, 32], P('narrow', 'wide'), may hold values from 1 to 128, as said below
Outputs:
- updated: float32 [16, 256, 32, 128], P('narrow', 'wide')
- residual: float32 [16, 256, 32, 128], P('narrow', 'wide')
Inputs may be any that keep to these rules, and one draw needn't show every extreme that they name: block_cols of a slot lies in the 3 x 3 neighbourhood of its block_rows position: with r = block_rows, c // 10 - r // 8 and c % 10 - r % 8 are each 0, 1 or 2. `live_count`: at least one tile uses all 128 slots.
All inputs are finite; a program needn't handle non-finite values.
Results may differ from a plain program's by a relative error of at most 0.0065.
Values may be sent and summed in bfloat16 or wider, within the bound.
No kernel may reach another device: no remote copies, remote signals or barrier semaphores. Data moves between devices by JAX's collectives and lax.ppermute only.
A program may use at most 64 MiB of HBM per device.

v0:
```python
import functools

import jax
import jax.numpy as jnp
from jax import lax
from jax.experimental import pallas as pl
from jax.experimental.pallas import tpu as pltpu
from jax.sharding import PartitionSpec as P

ITERS = 5
descent = 0.1

ROW_FIRST, ROW_LAST, COL_FIRST, COL_LAST, EVEN, ROW_EVEN, LIVE = range(7)


def cast_low(value):
    return value.astype(jnp.bfloat16)


def wide_value(value):
    return value.astype(jnp.float32)


def kept(value, drop):
    return jnp.where(drop, jnp.zeros_like(value), value)


def half_step(source_ref, parts, total_ref, source_ids, target_ids, live, filler=()):
    filler = list(filler)

    def add(first, blocks_ref):
        for at in range(0, blocks_ref.shape[0], 2):
            slot = first + at
            upper = source_ref[source_ids[slot]]
            lower = source_ref[source_ids[slot + 1]]
            frames, width = upper.shape
            zeros = jnp.zeros_like(upper)
            taken = jnp.concatenate(
                [jnp.concatenate([upper, zeros], axis=1), jnp.concatenate([zeros, lower], axis=1)],
                axis=0,
            )
            matrices = blocks_ref[pl.ds(at, 2)].reshape(2 * width, width)
            product = jnp.dot(taken, matrices, preferred_element_type=jnp.float32)
            target = target_ids[slot]
            total_ref[target] = total_ref[target] + product[:frames]
            target = target_ids[slot + 1]
            total_ref[target] = total_ref[target] + product[frames:]
            for work in filler[:2]:
                work()
            del filler[:2]

    first = 0
    for part in parts[:-1]:
        add(first, part)
        first += part.shape[0]
    for work in filler:
        work()
    filler.clear()

    @pl.when(live > first)
    def _():
        add(first, parts[-1])


def products(sizes, info_ref, rows_ref, cols_ref, observed_ref, blocks, turned, grad_ref, residual_ref, low_ref, rlow_ref):
    tile_x, tile_y, _ = sizes
    own = tile_x * tile_y
    extended = (tile_x + 2) * (tile_y + 2)
    low_ref[extended] = jnp.zeros_like(low_ref[extended])
    for block in range(own):
        residual_ref[block] = -observed_ref[block]
    residual_ref[own] = jnp.zeros_like(residual_ref[own])

    def clear(block):
        grad_ref[block] = jnp.zeros_like(grad_ref[block])

    clears = [functools.partial(clear, block) for block in range(extended + 1)]
    half_step(low_ref, blocks, residual_ref, cols_ref, rows_ref, info_ref[LIVE], clears)
    for block in range(own + 1):
        rlow_ref[block] = cast_low(residual_ref[block])
    half_step(rlow_ref, turned, grad_ref, rows_ref, cols_ref, info_ref[LIVE])


def send_columns(sizes, last, info_ref, grad_ref, pair_ref, next_ref):
    tile_x, tile_y, _ = sizes
    span = tile_y + 2
    even = info_ref[EVEN] == 1
    for out_ref, right in ((pair_ref, even), (next_ref, jnp.logical_not(even))):
        if last:
            col = jnp.where(right, span - 1, 0)
            for row in range(tile_x + 2):
                out_ref[row] = cast_low(grad_ref[row * span + col])
        else:
            col = jnp.where(right, span - 2, 0)
            for row in range(tile_x + 2):
                for step in range(2):
                    out_ref[row * 2 + step] = cast_low(grad_ref[row * span + col + step])


def outside(sizes, info_ref, row, col):
    tile_x, tile_y, _ = sizes
    flag = None
    for hit, place in (
        (row == 0, ROW_FIRST),
        (row == tile_x + 1, ROW_LAST),
        (col == 0, COL_FIRST),
        (col == tile_y + 1, COL_LAST),
    ):
        if hit:
            here = info_ref[place] == 1
            flag = here if flag is None else jnp.logical_or(flag, here)
    return flag


def came_along_wide(sizes, last, info_ref, pair_in, next_in, row, col):
    tile_x, tile_y, _ = sizes
    even = info_ref[EVEN] == 1
    width = 1 if last else 2
    lefts = {1: 0} if last else {0: 0, 1: 1}
    rights = {tile_y: 0} if last else {tile_y: 0, tile_y + 1: 1}
    for places, from_pair, place in (
        (lefts, jnp.logical_not(even), COL_FIRST),
        (rights, even, COL_LAST),
    ):
        if col in places:
            at = row * width + places[col]
            came = jnp.where(from_pair, pair_in[at], next_in[at])
            return kept(wide_value(came), info_ref[place] == 1)
    return None


def bring(blocks_in, blocks_ref, arrived, chunk, first):
    size = blocks_ref.shape[0] // arrived.shape[0]
    return pltpu.make_async_copy(
        blocks_in.at[pl.ds(first + chunk * size, size)],
        blocks_ref.at[pl.ds(chunk * size, size)],
        arrived.at[chunk],
    )


def plan_kernel(sizes, flags_ref, live_ref, rows_in, cols_in, info_ref, rows_ref, cols_ref):
    tile_x, tile_y, slots = sizes
    live = live_ref[0, 0]
    for place in range(LIVE):
        info_ref[place] = flags_ref[place]
    info_ref[LIVE] = live
    group = 8

    def copy(step, carry):
        for place in range(group):
            slot = step * group + place
            used = slot < live
            rows_ref[slot] = jnp.where(used, rows_in[slot], tile_x * tile_y)
            cols_ref[slot] = jnp.where(used, cols_in[slot], (tile_x + 2) * (tile_y + 2))
        return carry

    lax.fori_loop(0, slots // group, copy, 0)


def turn_kernel(info_ref, blocks_in, blocks_0, blocks_1, turned_0, turned_1, arrived_0, arrived_1):
    half = blocks_0.shape[0]
    chunks = arrived_0.shape[0]
    size = half // chunks
    more = info_ref[LIVE] > half
    for chunk in range(chunks):
        bring(blocks_in, blocks_0, arrived_0, chunk, 0).start()

    @pl.when(more)
    def _():
        for chunk in range(chunks):
            bring(blocks_in, blocks_1, arrived_1, chunk, half).start()

    for chunk in range(chunks):
        bring(blocks_in, blocks_0, arrived_0, chunk, 0).wait()
        for slot in range(chunk * size, (chunk + 1) * size):
            turned_0[slot] = blocks_0[slot].T

    @pl.when(more)
    def _():
        for chunk in range(chunks):
            bring(blocks_in, blocks_1, arrived_1, chunk, half).wait()
            for slot in range(chunk * size, (chunk + 1) * size):
                turned_1[slot] = blocks_1[slot].T


def first_kernel(sizes, info_ref, rows_ref, cols_ref, coef_ref, near_in, far_in, next_in, pair_in, observed_ref, blocks_0, blocks_1, turned_0, turned_1, x_ref, grad_ref, next_ref, pair_ref, low_ref, rlow_ref, residual_ref):
    tile_x, tile_y, _ = sizes
    span = tile_y + 2
    even = info_ref[EVEN] == 1
    for row in range(tile_x + 2):
        for col in range(span):
            if col == 0:
                value = wide_value(jnp.where(even, next_in[row], pair_in[row]))
            elif col == tile_y + 1:
                value = wide_value(jnp.where(even, pair_in[row], next_in[row]))
            elif row == 0:
                value = came_along_narrow(info_ref, near_in, far_in, True, col - 1)
            elif row == tile_x + 1:
                value = came_along_narrow(info_ref, near_in, far_in, False, col - 1)
            else:
                value = coef_ref[(row - 1) * tile_y + col - 1]
            drop = outside(sizes, info_ref, row, col)
            if drop is not None:
                value = kept(value, drop)
            x_ref[row * span + col] = value
            low_ref[row * span + col] = cast_low(value)
    products(sizes, info_ref, rows_ref, cols_ref, observed_ref, (blocks_0, blocks_1), (turned_0, turned_1), grad_ref, residual_ref, low_ref, rlow_ref)
    send_columns(sizes, False, info_ref, grad_ref, pair_ref, next_ref)


def step_kernel(sizes, last, info_ref, rows_ref, cols_ref, x_in, grad_in, next_in, pair_in, near_in, far_in, near_ends, far_ends, observed_ref, blocks_0, blocks_1, turned_0, turned_1, x_ref, grad_ref, next_ref, pair_ref, *rest):
    tile_x, tile_y, _ = sizes
    span = tile_y + 2
    even = info_ref[EVEN] == 1
    if last:
        residual_ref, low_ref, rlow_ref = rest
    else:
        low_ref, rlow_ref, residual_ref = rest
    for row in range(tile_x + 2):
        for col in range(span):
            at = row * span + col
            gradient = grad_in[at]
            came = came_along_wide(sizes, False, info_ref, pair_in, next_in, row, col)
            if came is not None:
                gradient = gradient + came
            if row < 2 or row >= tile_x:
                step = row if row < 2 else row - tile_x
                inner = step * (span - 2) + col
                if col < 2:
                    came = jnp.where(
                        even,
                        came_along_narrow(info_ref, near_ends, far_ends, row < 2, step * 2 + col),
                        came_along_narrow(info_ref, near_in, far_in, row < 2, inner),
                    )
                elif col >= span - 2:
                    end = step * 2 + col - span + 2
                    came = jnp.where(
                        even,
                        came_along_narrow(info_ref, near_in, far_in, row < 2, inner - 2),
                        came_along_narrow(info_ref, near_ends, far_ends, row < 2, end),
                    )
                else:
                    inner = jnp.where(even, inner - 2, inner)
                    came = came_along_narrow(info_ref, near_in, far_in, row < 2, inner)
                gradient = gradient + came
            value = x_in[at] - descent * gradient
            drop = outside(sizes, info_ref, row, col)
            if drop is not None:
                value = kept(value, drop)
            x_ref[at] = value
            low_ref[at] = cast_low(value)
    products(sizes, info_ref, rows_ref, cols_ref, observed_ref, (blocks_0, blocks_1), (turned_0, turned_1), grad_ref, residual_ref, low_ref, rlow_ref)
    send_columns(sizes, last, info_ref, grad_ref, pair_ref, next_ref)


def came_along_narrow(info_ref, near_in, far_in, upper, at):
    even = info_ref[ROW_EVEN] == 1
    from_near = jnp.logical_not(even) if upper else even
    came = jnp.where(from_near, near_in[at], far_in[at])
    return wide_value(kept(came, info_ref[ROW_FIRST if upper else ROW_LAST] == 1))


def shared_rows(sizes, info_ref, near_ref, far_ref):
    even = info_ref[ROW_EVEN] == 1
    lower = sizes[0]
    return ((near_ref, jnp.where(even, lower, 0)), (far_ref, jnp.where(even, 0, lower)))


def inner_kernel(sizes, info_ref, grad_in, pair_in, near_ref, far_ref):
    span = sizes[1] + 2
    even = info_ref[EVEN] == 1
    first = jnp.where(even, 2, 0)
    for out_ref, start in shared_rows(sizes, info_ref, near_ref, far_ref):
        for step in range(2):
            row = start + step
            for place in range(span - 2):
                value = grad_in[row * span + first + place]
                if place < 2:
                    value = value + wide_value(kept(pair_in[row * 2 + place], even))
                elif place >= span - 4:
                    came = pair_in[row * 2 + place - span + 4]
                    value = value + wide_value(kept(came, jnp.logical_not(even)))
                out_ref[step * (span - 2) + place] = cast_low(value)


def ends_kernel(sizes, info_ref, grad_in, next_in, near_ref, far_ref):
    span = sizes[1] + 2
    even = info_ref[EVEN] == 1
    first = jnp.where(even, 0, span - 2)
    nobody = jnp.where(even, info_ref[COL_FIRST], info_ref[COL_LAST]) == 1
    for out_ref, start in shared_rows(sizes, info_ref, near_ref, far_ref):
        for step in range(2):
            row = start + step
            for place in range(2):
                value = grad_in[row * span + first + place]
                value = value + wide_value(kept(next_in[row * 2 + place], nobody))
                out_ref[step * 2 + place] = cast_low(value)


def last_kernel(sizes, info_ref, grad_in, next_in, pair_in, near_ref, far_ref):
    tile_x, tile_y, _ = sizes
    span = tile_y + 2
    even = info_ref[ROW_EVEN] == 1
    for out_ref, lower in ((near_ref, even), (far_ref, jnp.logical_not(even))):
        row = jnp.where(lower, tile_x + 1, 0)
        for col in range(1, tile_y + 1):
            value = grad_in[row * span + col]
            came = came_along_wide(sizes, True, info_ref, pair_in, next_in, row, col)
            out_ref[col - 1] = cast_low(value if came is None else value + came)


def final_kernel(sizes, rows, info_ref, x_in, grad_in, next_in, pair_in, *rest):
    tile_x, tile_y, _ = sizes
    span = tile_y + 2
    if len(rest) > 3:
        near_in, far_in, _, out_ref, part_ref, sent = rest
    else:
        out_ref, part_ref, sent = rest
    copies = []
    for place, row in enumerate(rows):
        for col in range(1, tile_y + 1):
            at = row * span + col
            gradient = grad_in[at]
            came = came_along_wide(sizes, True, info_ref, pair_in, next_in, row, col)
            if came is not None:
                gradient = gradient + came
            if row == 1:
                gradient = gradient + came_along_narrow(info_ref, near_in, far_in, True, col - 1)
            if row == tile_x:
                gradient = gradient + came_along_narrow(info_ref, near_in, far_in, False, col - 1)
            part_ref[place, col - 1] = x_in[at] - descent * gradient
        copies.append(pltpu.make_async_copy(part_ref.at[place], out_ref.at[row - 1], sent.at[place]))
        copies[-1].start()
    for copy in copies:
        copy.wait()


def local(coefficients, observed, blocks, block_rows, block_cols, live_count):
    tile_x, tile_y, frames, width = coefficients.shape
    slots = blocks.shape[2]
    own = tile_x * tile_y
    span = tile_y + 2
    extended = (tile_x + 2) * span
    sizes = (tile_x, tile_y, slots)
    narrow = lax.axis_size("narrow")
    wide = lax.axis_size("wide")
    a = lax.axis_index("narrow")
    b = lax.axis_index("wide")
    flags = jnp.stack([a == 0, a == narrow - 1, b == 0, b == wide - 1, b % 2 == 0, a % 2 == 0]).astype(jnp.int32)
    even = b % 2 == 0
    row_even = a % 2 == 0

    def everywhere(move):
        return [
            (i * narrow + j, to_i * narrow + to_j)
            for i in range(wide)
            for j in range(narrow)
            for to_i, to_j in [move(i, j)]
        ]

    def other(i, j):
        return (i, j ^ 1) if i in (0, wide - 1) else (((i - 1) ^ 1) + 1, j)

    def far(i, j):
        return (i ^ 1, j) if j in (0, narrow - 1) else (i, ((j - 1) ^ 1) + 1)

    near_pairs = everywhere(lambda i, j: (i, j ^ 1))
    far_pairs = everywhere(far)
    pairs = everywhere(lambda i, j: (i ^ 1, j))
    others = everywhere(other)

    def send(value, ring):
        return lax.ppermute(value, ("wide", "narrow"), ring)

    def along_narrow(near, far):
        return send(near, near_pairs), send(far, far_pairs)

    def along_wide(other, pair):
        return send(other, others), send(pair, pairs)

    seen = observed.reshape(own, frames, width)

    smem = pl.BlockSpec(memory_space=pltpu.SMEM)
    vmem = pl.BlockSpec(memory_space=pltpu.VMEM)

    def shape(count, kind):
        return jax.ShapeDtypeStruct((count, frames, width), kind)

    def place(output):
        return vmem if len(output.shape) > 1 else smem

    def call(kernel, name, inputs, scalars, outputs, scratch=(), flops=0):
        return pl.pallas_call(
            kernel,
            out_shape=outputs,
            in_specs=[smem] * scalars + [vmem] * (len(inputs) - scalars),
            out_specs=jax.tree.map(place, outputs),
            scratch_shapes=list(scratch),
            compiler_params=pltpu.CompilerParams(vmem_limit_bytes=24 << 20),
            cost_estimate=pl.CostEstimate(flops=flops, bytes_accessed=1 << 20, transcendentals=0),
            name=name,
        )(*inputs)

    low_scratch = pltpu.VMEM((extended + 1, frames, width), jnp.bfloat16)
    rlow_scratch = pltpu.VMEM((own + 1, frames, width), jnp.bfloat16)
    residual_scratch = pltpu.VMEM((own + 1, frames, width), jnp.float32)
    work = 4 * slots * frames * width * width

    def step_outputs(last):
        sent = tile_x + 2 if last else 2 * (tile_x + 2)
        outputs = [
            shape(extended, jnp.float32),
            shape(extended + 1, jnp.float32),
            shape(sent, jnp.bfloat16),
            shape(sent, jnp.bfloat16),
        ]
        if last:
            return outputs + [shape(own + 1, jnp.float32)]
        return outputs

    top, bottom = lax.optimization_barrier((coefficients[0], coefficients[tile_x - 1]))
    near, far_row = lax.optimization_barrier(
        (cast_low(jnp.where(row_even, bottom, top)), cast_low(jnp.where(row_even, top, bottom)))
    )
    near, far_row = along_narrow(near, far_row)
    in_hbm = pltpu.with_memory_space_constraint
    info, row_ids, col_ids = pl.pallas_call(
        functools.partial(plan_kernel, sizes),
        out_shape=[
            pltpu.SMEM((LIVE + 1,), jnp.int32),
            pltpu.SMEM((slots,), jnp.int32),
            pltpu.SMEM((slots,), jnp.int32),
        ],
        in_specs=[smem] * 4,
        out_specs=[smem] * 3,
        compiler_params=pltpu.CompilerParams(vmem_limit_bytes=24 << 20),
        cost_estimate=pl.CostEstimate(flops=work, bytes_accessed=1 << 20, transcendentals=0),
        name="plan_slots",
    )(
        flags,
        live_count,
        in_hbm(block_rows.reshape(slots), pltpu.HBM),
        in_hbm(block_cols.reshape(slots), pltpu.HBM),
    )
    chunks = 4
    half_shape = pltpu.VMEM((slots // 2, width, width), jnp.bfloat16)
    operator = pl.pallas_call(
        turn_kernel,
        out_shape=[half_shape] * 4,
        in_specs=[smem, pl.BlockSpec(memory_space=pltpu.HBM)],
        out_specs=[vmem] * 4,
        scratch_shapes=[pltpu.SemaphoreType.DMA((chunks,))] * 2,
        compiler_params=pltpu.CompilerParams(vmem_limit_bytes=24 << 20),
        cost_estimate=pl.CostEstimate(flops=work, bytes_accessed=4 << 20, transcendentals=0),
        name="turn_blocks",
    )(info, in_hbm(blocks.reshape(slots, width, width), pltpu.HBM))
    near, far_row, info = lax.optimization_barrier((near, far_row, info))
    above = jnp.where(row_even, far_row, near)
    below = jnp.where(row_even, near, far_row)
    left, right = lax.optimization_barrier((coefficients[:, 0], coefficients[:, tile_y - 1]))
    left, right = cast_low(left), cast_low(right)
    sides = []
    for col, edge in ((0, left), (tile_y - 1, right)):
        sides.append(jnp.concatenate([above[col : col + 1], edge, below[col : col + 1]], axis=0))
    next_out, pair_out = lax.optimization_barrier(
        (jnp.where(even, sides[0], sides[1]), jnp.where(even, sides[1], sides[0]))
    )
    next_in, pair_in = along_wide(next_out, pair_out)
    x, grad, next_out, pair_out = call(
        functools.partial(first_kernel, sizes),
        "first_step",
        [info, row_ids, col_ids, coefficients.reshape(own, frames, width), near, far_row, next_in, pair_in, seen, *operator],
        3,
        step_outputs(False),
        [low_scratch, rlow_scratch, residual_scratch],
        work,
    )
    for iteration in range(ITERS):
        last = iteration == ITERS - 1
        next_in, pair_in = along_wide(next_out, pair_out)
        if last:
            folds = [(last_kernel, "rows_beyond", [next_in, pair_in], tile_y)]
        else:
            folds = [
                (inner_kernel, "inner_columns", [pair_in], 2 * (span - 2)),
                (ends_kernel, "end_columns", [next_in], 4),
            ]
        came = []
        for kernel, name, wide_in, count in folds:
            near, far_row = call(
                functools.partial(kernel, sizes),
                name,
                [info, grad, *wide_in],
                1,
                [shape(count, jnp.bfloat16)] * 2,
            )
            came += along_narrow(near, far_row)
        if last:
            inner = list(range(2, tile_x))
            outer = [1, tile_x]
            stay = pl.BlockSpec(memory_space=pltpu.HBM)
            inputs = [info, x, grad, next_in, pair_in]

            def final_call(rows, operands, aliases, name):
                specs = [smem] + [vmem] * (len(operands) - 1)
                if aliases:
                    specs[-1] = stay
                return pl.pallas_call(
                    functools.partial(final_kernel, sizes, rows),
                    out_shape=jax.ShapeDtypeStruct(coefficients.shape, jnp.float32),
                    in_specs=specs,
                    out_specs=stay,
                    scratch_shapes=[
                        pltpu.VMEM((len(rows), tile_y, frames, width), jnp.float32),
                        pltpu.SemaphoreType.DMA((len(rows),)),
                    ],
                    input_output_aliases=aliases,
                    compiler_params=pltpu.CompilerParams(vmem_limit_bytes=24 << 20),
                    cost_estimate=pl.CostEstimate(flops=work, bytes_accessed=1 << 20, transcendentals=0),
                    name=name,
                )(*operands)

            started = final_call(inner, inputs, {}, "inner_rows")
            updated = final_call(outer, inputs + [*came, started], {7: 0}, "outer_rows")
        else:
            ending = iteration == ITERS - 2
            x, grad, next_out, pair_out, *rest = call(
                functools.partial(step_kernel, sizes, ending),
                "one_step",
                [info, row_ids, col_ids, x, grad, next_in, pair_in, *came, seen, *operator],
                3,
                step_outputs(ending),
                [low_scratch, rlow_scratch] + ([] if ending else [residual_scratch]),
                work,
            )
    residual = rest[0]
    return (
        updated,
        residual[:own].reshape(coefficients.shape),
    )


def solution(mesh):
    placed = (
        P("narrow", "wide", None, None),
        P("narrow", "wide", None, None),
        P("narrow", "wide", None, None, None),
        P("narrow", "wide", None),
        P("narrow", "wide", None),
        P("narrow", "wide"),
    )
    return jax.shard_map(
        local,
        mesh=mesh,
        in_specs=placed,
        out_specs=(P("narrow", "wide", None, None), P("narrow", "wide", None, None)),
        check_vma=False,
    )
```

profile of v0, /device:TPU:26, one launch (start us, length us, event | category | flops | bytes accessed | tf_op | source)
XLA Modules:
  0.0 74.0 jit_solution(15734205614039600905)
XLA Ops:
  0.6 1.0 %slice_bitcast_fusion = (bf16[8,32,128]{2,1,0:T(8,128)(2,1)S(1)}, bf16[8,32,128]{2,1,0:T(8,128)(2,1)S(1)}) fusion(f32[4,8,32,128]{3,2,1,0:T(8,128)} %param.6), kind=kLoop, calls=%fused_computation.2 | loop fusion | bytes 262144 | tf_op jit(solution)/shard_map/squeeze | solution.py:421
  1.7 0.6 collective-permute-start
  2.3 2.2 %collective-permute-start.1 = (bf16[8,32,128]{2,1,0:T(8,128)(2,1)S(1)}, bf16[8,32,128]{2,1,0:T(8,128)(2,1)S(1)}, u32[]{:S(2)}, u32[]{:S(2)}) collective-permute-start(bf16[8,32,128]{2,1,0:T(8,128)(2,1)S(1)} %get-tuple-element.62), channel_id=1, source_target_pairs={{0,4},{1,2},{2,1},{3,7},{4,0},{5,6},{6,5},{7,3},{8,12},{9,10},{10,... | collective-permute-start | bytes 196616 | tf_op jit(solution)/shard_map/ppermute | solution.py:373
  4.4 0.9 %slice_bitcast_fusion.2 = (bf16[4,32,128]{2,1,0:T(8,128)(2,1)S(1)}, bf16[4,32,128]{2,1,0:T(8,128)(2,1)S(1)}) fusion(f32[4,8,32,128]{3,2,1,0:T(8,128)} %param.6), kind=kLoop, calls=%fused_computation.4 | loop fusion | bytes 131072 | tf_op jit(solution)/shard_map/squeeze | solution.py:460
  6.1 1.1 %plan_slots.1 = (s32[7]{0:T(128)S(4)}, s32[128]{0:T(128)S(4)}, s32[128]{0:T(128)S(4)}) custom-call(s32[6]{0:T(128)S(1)} %convert_element_type.17.flags_ref, s32[1,1]{1,0:T(1,128)S(6)} %copy.14.live_ref, s32[128]{0:T(128)} %bitcast.32, s32[128]{0:T(128)} %bitcast.33), custom_call_target="tpu_custom_call" | custom-call | flops 268435456 | bytes 1048576 | tf_op jit(solution)/shard_map/plan_slots/pallas_call | solution.py:427
  7.3 3.2 %collective-permute-start.2 = (bf16[6,32,128]{2,1,0:T(8,128)(2,1)S(1)}, bf16[6,32,128]{2,1,0:T(8,128)(2,1)S(1)}, u32[]{:S(2)}, u32[]{:S(2)}) collective-permute-start(bf16[6,32,128]{2,1,0:T(8,128)(2,1)S(1)} %get-tuple-element.71), channel_id=1, source_target_pairs={{0,1},{1,0},{2,3},{3,2},{4,8},{5,9},{6,10},{7,11},{8,4},{9,5},{10,... | collective-permute-start | bytes 147464 | tf_op jit(solution)/shard_map/ppermute | solution.py:373
  10.5 2.0 %turn_blocks.1 = (bf16[64,128,128]{2,1,0:T(8,128)(2,1)S(1)}, bf16[64,128,128]{2,1,0:T(8,128)(2,1)S(1)}, bf16[64,128,128]{2,1,0:T(8,128)(2,1)S(1)}, bf16[64,128,128]{2,1,0:T(8,128)(2,1)S(1)}) custom-call(s32[7]{0:T(128)S(4)} %get-tuple-element.64.info_ref, bf16[128,128,128]{2,1,0:T(8,128)(2,1)} %bitcast.30), custom_call_target="tpu_custom_call" | custom-call | flops 268435456 | bytes 4194304 | tf_op jit(solution)/shard_map/turn_blocks/pallas_call | solution.py:447
  12.4 0.6 collective-permute-done.2.next_in
  13.0 1.3 %first_step.1 = (f32[60,32,128]{2,1,0:T(8,128)S(1)}, f32[61,32,128]{2,1,0:T(8,128)S(1)}, bf16[12,32,128]{2,1,0:T(8,128)(2,1)S(1)}, bf16[12,32,128]{2,1,0:T(8,128)(2,1)S(1)}) custom-call(s32[7]{0:T(128)S(4)} %get-tuple-element.64.info_ref, s32[128]{0:T(128)S(4)} %get-tuple-element.65.rows_ref, s32[128]{0:T(128)S(4)} %get-tuple-element.66.cols_ref, ...), custom_call_target="tpu_custom_call" | custom-call | flops 268435456 | bytes 1048576 | tf_op jit(solution)/shard_map/first_step/pallas_call | solution.py:393
  14.4 3.2 %collective-permute-start.4 = (bf16[12,32,128]{2,1,0:T(8,128)(2,1)S(1)}, bf16[12,32,128]{2,1,0:T(8,128)(2,1)S(1)}, u32[]{:S(2)}, u32[]{:S(2)}) collective-permute-start(bf16[12,32,128]{2,1,0:T(8,128)(2,1)S(1)} %get-tuple-element.79), channel_id=1, source_target_pairs={{0,1},{1,0},{2,3},{3,2},{4,8},{5,9},{6,10},{7,11},{8,4},{9,5},{10,... | collective-permute-start | bytes 294920 | tf_op jit(solution)/shard_map/ppermute | solution.py:373
  17.7 0.6 collective-permute-start.6
  18.3 1.6 %collective-permute-start.7 = (bf16[16,32,128]{2,1,0:T(8,128)(2,1)S(1)}, bf16[16,32,128]{2,1,0:T(8,128)(2,1)S(1)}, u32[]{:S(2)}, u32[]{:S(2)}) collective-permute-start(bf16[16,32,128]{2,1,0:T(8,128)(2,1)S(1)} %get-tuple-element.82), channel_id=1, source_target_pairs={{0,4},{1,2},{2,1},{3,7},{4,0},{5,6},{6,5},{7,3},{8,12},{9,10},{10,... | collective-permute-start | bytes 393224 | tf_op jit(solution)/shard_map/ppermute | solution.py:373
  19.9 0.8 %collective-permute-done.4.next_in = bf16[12,32,128]{2,1,0:T(8,128)(2,1)S(1)} collective-permute-done((bf16[12,32,128]{2,1,0:T(8,128)(2,1)S(1)}, bf16[12,32,128]{2,1,0:T(8,128)(2,1)S(1)}, u32[]{:S(2)}, u32[]{:S(2)}) %collective-permute-start.4) | collective-permute-done | bytes 98336 | tf_op jit(solution)/shard_map/ppermute | solution.py:373
  20.7 0.6 collective-permute-start.8
  21.3 1.5 %collective-permute-start.9 = (bf16[4,32,128]{2,1,0:T(8,128)(2,1)S(1)}, bf16[4,32,128]{2,1,0:T(8,128)(2,1)S(1)}, u32[]{:S(2)}, u32[]{:S(2)}) collective-permute-start(bf16[4,32,128]{2,1,0:T(8,128)(2,1)S(1)} %get-tuple-element.84), channel_id=1, source_target_pairs={{0,4},{1,2},{2,1},{3,7},{4,0},{5,6},{6,5},{7,3},{8,12},{9,10},{10,... | collective-permute-start | bytes 98312 | tf_op jit(solution)/shard_map/ppermute | solution.py:373
  22.8 1.9 %collective-permute-done.8.near_ends = bf16[4,32,128]{2,1,0:T(8,128)(2,1)S(1)} collective-permute-done((bf16[4,32,128]{2,1,0:T(8,128)(2,1)S(1)}, bf16[4,32,128]{2,1,0:T(8,128)(2,1)S(1)}, u32[]{:S(2)}, u32[]{:S(2)}) %collective-permute-start.8) | collective-permute-done | bytes 32800 | tf_op jit(solution)/shard_map/ppermute | solution.py:373
  24.7 0.5 collective-permute-done.9.far_ends
  25.2 1.6 %one_step.4 = (f32[60,32,128]{2,1,0:T(8,128)S(1)}, f32[61,32,128]{2,1,0:T(8,128)S(1)}, bf16[12,32,128]{2,1,0:T(8,128)(2,1)S(1)}, bf16[12,32,128]{2,1,0:T(8,128)(2,1)S(1)}) custom-call(s32[7]{0:T(128)S(4)} %get-tuple-element.64.info_ref, s32[128]{0:T(128)S(4)} %get-tuple-element.65.rows_ref, s32[128]{0:T(128)S(4)} %get-tuple-element.66.cols_ref, ...), custom_call_target="tpu_custom_call" | custom-call | flops 268435456 | bytes 1048576 | tf_op jit(solution)/shard_map/one_step/pallas_call | solution.py:393
  26.9 1.8 %collective-permute-start.10 = (bf16[12,32,128]{2,1,0:T(8,128)(2,1)S(1)}, bf16[12,32,128]{2,1,0:T(8,128)(2,1)S(1)}, u32[]{:S(2)}, u32[]{:S(2)}) collective-permute-start(bf16[12,32,128]{2,1,0:T(8,128)(2,1)S(1)} %get-tuple-element.87), channel_id=1, source_target_pairs={{0,1},{1,0},{2,3},{3,2},{4,8},{5,9},{6,10},{7,11},{8,4},{9,5},{10,... | collective-permute-start | bytes 294920 | tf_op jit(solution)/shard_map/ppermute | solution.py:373
  28.7 0.3 collective-permute-start.12
  29.0 1.7 %collective-permute-start.13 = (bf16[16,32,128]{2,1,0:T(8,128)(2,1)S(1)}, bf16[16,32,128]{2,1,0:T(8,128)(2,1)S(1)}, u32[]{:S(2)}, u32[]{:S(2)}) collective-permute-start(bf16[16,32,128]{2,1,0:T(8,128)(2,1)S(1)} %get-tuple-element.90), channel_id=1, source_target_pairs={{0,4},{1,2},{2,1},{3,7},{4,0},{5,6},{6,5},{7,3},{8,12},{9,10},{10,... | collective-permute-start | bytes 393224 | tf_op jit(solution)/shard_map/ppermute | solution.py:373
  30.7 2.4 %collective-permute-done.10.next_in = bf16[12,32,128]{2,1,0:T(8,128)(2,1)S(1)} collective-permute-done((bf16[12,32,128]{2,1,0:T(8,128)(2,1)S(1)}, bf16[12,32,128]{2,1,0:T(8,128)(2,1)S(1)}, u32[]{:S(2)}, u32[]{:S(2)}) %collective-permute-start.10) | collective-permute-done | bytes 98336 | tf_op jit(solution)/shard_map/ppermute | solution.py:373
  33.1 0.1 collective-permute-start.14
  33.2 1.6 %collective-permute-start.15 = (bf16[4,32,128]{2,1,0:T(8,128)(2,1)S(1)}, bf16[4,32,128]{2,1,0:T(8,128)(2,1)S(1)}, u32[]{:S(2)}, u32[]{:S(2)}) collective-permute-start(bf16[4,32,128]{2,1,0:T(8,128)(2,1)S(1)} %get-tuple-element.92), channel_id=1, source_target_pairs={{0,4},{1,2},{2,1},{3,7},{4,0},{5,6},{6,5},{7,3},{8,12},{9,10},{10,... | collective-permute-start | bytes 98312 | tf_op jit(solution)/shard_map/ppermute | solution.py:373
  34.9 2.2 %collective-permute-done.14.near_ends = bf16[4,32,128]{2,1,0:T(8,128)(2,1)S(1)} collective-permute-done((bf16[4,32,128]{2,1,0:T(8,128)(2,1)S(1)}, bf16[4,32,128]{2,1,0:T(8,128)(2,1)S(1)}, u32[]{:S(2)}, u32[]{:S(2)}) %collective-permute-start.14) | collective-permute-done | bytes 32800 | tf_op jit(solution)/shard_map/ppermute | solution.py:373
  37.2 1.7 %one_step.5 = (f32[60,32,128]{2,1,0:T(8,128)S(1)}, f32[61,32,128]{2,1,0:T(8,128)S(1)}, bf16[12,32,128]{2,1,0:T(8,128)(2,1)S(1)}, bf16[12,32,128]{2,1,0:T(8,128)(2,1)S(1)}) custom-call(s32[7]{0:T(128)S(4)} %get-tuple-element.64.info_ref, s32[128]{0:T(128)S(4)} %get-tuple-element.65.rows_ref, s32[128]{0:T(128)S(4)} %get-tuple-element.66.cols_ref, ...), custom_call_target="tpu_custom_call" | custom-call | flops 268435456 | bytes 1048576 | tf_op jit(solution)/shard_map/one_step/pallas_call | solution.py:393
  39.0 0.7 collective-permute-start.16
  39.7 0.6 collective-permute-done.17.pair_in
  40.4 0.1 collective-permute-start.18
  40.5 1.7 %collective-permute-start.19 = (bf16[16,32,128]{2,1,0:T(8,128)(2,1)S(1)}, bf16[16,32,128]{2,1,0:T(8,128)(2,1)S(1)}, u32[]{:S(2)}, u32[]{:S(2)}) collective-permute-start(bf16[16,32,128]{2,1,0:T(8,128)(2,1)S(1)} %get-tuple-element.98), channel_id=1, source_target_pairs={{0,4},{1,2},{2,1},{3,7},{4,0},{5,6},{6,5},{7,3},{8,12},{9,10},{10,... | collective-permute-start | bytes 393224 | tf_op jit(solution)/shard_map/ppermute | solution.py:373
  42.2 3.1 %collective-permute-done.16.next_in = bf16[12,32,128]{2,1,0:T(8,128)(2,1)S(1)} collective-permute-done((bf16[12,32,128]{2,1,0:T(8,128)(2,1)S(1)}, bf16[12,32,128]{2,1,0:T(8,128)(2,1)S(1)}, u32[]{:S(2)}, u32[]{:S(2)}) %collective-permute-start.16) | collective-permute-done | bytes 98336 | tf_op jit(solution)/shard_map/ppermute | solution.py:373
  45.3 0.1 collective-permute-start.20
  45.4 1.7 %collective-permute-start.21 = (bf16[4,32,128]{2,1,0:T(8,128)(2,1)S(1)}, bf16[4,32,128]{2,1,0:T(8,128)(2,1)S(1)}, u32[]{:S(2)}, u32[]{:S(2)}) collective-permute-start(bf16[4,32,128]{2,1,0:T(8,128)(2,1)S(1)} %get-tuple-element.100), channel_id=1, source_target_pairs={{0,4},{1,2},{2,1},{3,7},{4,0},{5,6},{6,5},{7,3},{8,12},{9,10},{10,... | collective-permute-start | bytes 98312 | tf_op jit(solution)/shard_map/ppermute | solution.py:373
  47.1 2.2 %collective-permute-done.20.near_ends = bf16[4,32,128]{2,1,0:T(8,128)(2,1)S(1)} collective-permute-done((bf16[4,32,128]{2,1,0:T(8,128)(2,1)S(1)}, bf16[4,32,128]{2,1,0:T(8,128)(2,1)S(1)}, u32[]{:S(2)}, u32[]{:S(2)}) %collective-permute-start.20) | collective-permute-done | bytes 32800 | tf_op jit(solution)/shard_map/ppermute | solution.py:373
  49.4 1.6 %one_step.6 = (f32[60,32,128]{2,1,0:T(8,128)S(1)}, f32[61,32,128]{2,1,0:T(8,128)S(1)}, bf16[12,32,128]{2,1,0:T(8,128)(2,1)S(1)}, bf16[12,32,128]{2,1,0:T(8,128)(2,1)S(1)}) custom-call(s32[7]{0:T(128)S(4)} %get-tuple-element.64.info_ref, s32[128]{0:T(128)S(4)} %get-tuple-element.65.rows_ref, s32[128]{0:T(128)S(4)} %get-tuple-element.66.cols_ref, ...), custom_call_target="tpu_custom_call" | custom-call | flops 268435456 | bytes 1048576 | tf_op jit(solution)/shard_map/one_step/pallas_call | solution.py:393
  51.0 0.3 collective-permute-start.22
  51.3 1.0 %collective-permute-done.23.pair_in = bf16[12,32,128]{2,1,0:T(8,128)(2,1)S(1)} collective-permute-done((bf16[12,32,128]{2,1,0:T(8,128)(2,1)S(1)}, bf16[12,32,128]{2,1,0:T(8,128)(2,1)S(1)}, u32[]{:S(2)}, u32[]{:S(2)}) %collective-permute-start.23) | collective-permute-done | bytes 98336 | tf_op jit(solution)/shard_map/ppermute | solution.py:373
  52.5 1.8 %collective-permute-start.25 = (bf16[16,32,128]{2,1,0:T(8,128)(2,1)S(1)}, bf16[16,32,128]{2,1,0:T(8,128)(2,1)S(1)}, u32[]{:S(2)}, u32[]{:S(2)}) collective-permute-start(bf16[16,32,128]{2,1,0:T(8,128)(2,1)S(1)} %get-tuple-element.106), channel_id=1, source_target_pairs={{0,4},{1,2},{2,1},{3,7},{4,0},{5,6},{6,5},{7,3},{8,12},{9,10},{10,... | collective-permute-start | bytes 393224 | tf_op jit(solution)/shard_map/ppermute | solution.py:373
  54.3 3.0 %collective-permute-done.22.next_in = bf16[12,32,128]{2,1,0:T(8,128)(2,1)S(1)} collective-permute-done((bf16[12,32,128]{2,1,0:T(8,128)(2,1)S(1)}, bf16[12,32,128]{2,1,0:T(8,128)(2,1)S(1)}, u32[]{:S(2)}, u32[]{:S(2)}) %collective-permute-start.22) | collective-permute-done | bytes 98336 | tf_op jit(solution)/shard_map/ppermute | solution.py:373
  57.4 1.8 %collective-permute-start.27 = (bf16[4,32,128]{2,1,0:T(8,128)(2,1)S(1)}, bf16[4,32,128]{2,1,0:T(8,128)(2,1)S(1)}, u32[]{:S(2)}, u32[]{:S(2)}) collective-permute-start(bf16[4,32,128]{2,1,0:T(8,128)(2,1)S(1)} %get-tuple-element.108), channel_id=1, source_target_pairs={{0,4},{1,2},{2,1},{3,7},{4,0},{5,6},{6,5},{7,3},{8,12},{9,10},{10,... | collective-permute-start | bytes 98312 | tf_op jit(solution)/shard_map/ppermute | solution.py:373
  59.2 2.1 %collective-permute-done.26.near_ends = bf16[4,32,128]{2,1,0:T(8,128)(2,1)S(1)} collective-permute-done((bf16[4,32,128]{2,1,0:T(8,128)(2,1)S(1)}, bf16[4,32,128]{2,1,0:T(8,128)(2,1)S(1)}, u32[]{:S(2)}, u32[]{:S(2)}) %collective-permute-start.26) | collective-permute-done | bytes 32800 | tf_op jit(solution)/shard_map/ppermute | solution.py:373
  61.4 1.5 %one_step.7 = (f32[60,32,128]{2,1,0:T(8,128)S(1)}, f32[61,32,128]{2,1,0:T(8,128)S(1)}, bf16[6,32,128]{2,1,0:T(8,128)(2,1)S(1)}, bf16[6,32,128]{2,1,0:T(8,128)(2,1)S(1)}, f32[33,32,128]{2,1,0:T(8,128)S(1)}) custom-call(s32[7]{0:T(128)S(4)} %get-tuple-element.64.info_ref, s32[128]{0:T(128)S(4)} %get-tuple-element.65.rows_ref, ...), custom_call_target="tpu_custom_call" | custom-call | flops 268435456 | bytes 1048576 | tf_op jit(solution)/shard_map/one_step/pallas_call | solution.py:393
  63.1 5.5 %collective-permute-done.28.next_in = bf16[6,32,128]{2,1,0:T(8,128)(2,1)S(1)} collective-permute-done((bf16[6,32,128]{2,1,0:T(8,128)(2,1)S(1)}, bf16[6,32,128]{2,1,0:T(8,128)(2,1)S(1)}, u32[]{:S(2)}, u32[]{:S(2)}) %collective-permute-start.28) | collective-permute-done | bytes 49184 | tf_op jit(solution)/shard_map/ppermute | solution.py:373
  68.8 1.9 %collective-permute-start.31 = (bf16[8,32,128]{2,1,0:T(8,128)(2,1)S(1)}, bf16[8,32,128]{2,1,0:T(8,128)(2,1)S(1)}, u32[]{:S(2)}, u32[]{:S(2)}) collective-permute-start(bf16[8,32,128]{2,1,0:T(8,128)(2,1)S(1)} %get-tuple-element.114), channel_id=1, source_target_pairs={{0,4},{1,2},{2,1},{3,7},{4,0},{5,6},{6,5},{7,3},{8,12},{9,10},{10,... | collective-permute-start | bytes 196616 | tf_op jit(solution)/shard_map/ppermute | solution.py:373
  70.6 0.8 %slice.35 = f32[32,32,128]{2,1,0:T(8,128)} slice(f32[33,32,128]{2,1,0:T(8,128)S(1)} %get-tuple-element.115), slice={[0:32], [0:32], [0:128]} | slice | bytes 1048576 | tf_op jit(solution)/shard_map/slice | solution.py:539
  71.5 0.7 inner_rows.1.rest_2_
  72.2 0.8 %collective-permute-done.30.rest_0_ = bf16[8,32,128]{2,1,0:T(8,128)(2,1)S(1)} collective-permute-done((bf16[8,32,128]{2,1,0:T(8,128)(2,1)S(1)}, bf16[8,32,128]{2,1,0:T(8,128)(2,1)S(1)}, u32[]{:S(2)}, u32[]{:S(2)}) %collective-permute-start.30) | collective-permute-done | bytes 65568 | tf_op jit(solution)/shard_map/ppermute | solution.py:373
  73.1 0.8 %outer_rows.1 = f32[4,8,32,128]{3,2,1,0:T(8,128)} custom-call(s32[7]{0:T(128)S(4)} %get-tuple-element.64.info_ref, f32[60,32,128]{2,1,0:T(8,128)S(1)} %get-tuple-element.109.x_in, f32[61,32,128]{2,1,0:T(8,128)S(1)} %get-tuple-element.110.grad_in, bf16[6,32,128]{2,1,0:T(8,128)(2,1)S(1)} %collective-permute-done.28.next_in, ...), custom_call_target="tpu_custom_call", output_to_operand_aliasing={{}: (7, {})} | custom-call | flops 268435456 | bytes 1048576 | tf_op jit(solution)/shard_map/outer_rows/pallas_call | solution.py:508
  (47 shorter events, 1.6 us)
Async XLA Ops:
  1.7 5.5 %collective-permute-start = (bf16[8,32,128]{2,1,0:T(8,128)(2,1)S(1)}, bf16[8,32,128]{2,1,0:T(8,128)(2,1)S(1)}, u32[]{:S(2)}, u32[]{:S(2)}) collective-permute-start(bf16[8,32,128]{2,1,0:T(8,128)(2,1)S(1)} %get-tuple-element.61), channel_id=1, source_target_pairs={{0,1},{1,0},{2,3},{3,2},{4,5},{5,4},{6,7},{7,6},{8,9},{9,8},{10,11... | collective-permute-start | bytes 196616 | tf_op jit(solution)/shard_map/ppermute | solution.py:373
  2.3 4.9 %collective-permute-start.1 = (bf16[8,32,128]{2,1,0:T(8,128)(2,1)S(1)}, bf16[8,32,128]{2,1,0:T(8,128)(2,1)S(1)}, u32[]{:S(2)}, u32[]{:S(2)}) collective-permute-start(bf16[8,32,128]{2,1,0:T(8,128)(2,1)S(1)} %get-tuple-element.62), channel_id=1, source_target_pairs={{0,4},{1,2},{2,1},{3,7},{4,0},{5,6},{6,5},{7,3},{8,12},{9,10},{10,... | collective-permute-start | bytes 196616 | tf_op jit(solution)/shard_map/ppermute | solution.py:373
  7.3 5.7 %collective-permute-start.2 = (bf16[6,32,128]{2,1,0:T(8,128)(2,1)S(1)}, bf16[6,32,128]{2,1,0:T(8,128)(2,1)S(1)}, u32[]{:S(2)}, u32[]{:S(2)}) collective-permute-start(bf16[6,32,128]{2,1,0:T(8,128)(2,1)S(1)} %get-tuple-element.71), channel_id=1, source_target_pairs={{0,1},{1,0},{2,3},{3,2},{4,8},{5,9},{6,10},{7,11},{8,4},{9,5},{10,... | collective-permute-start | bytes 147464 | tf_op jit(solution)/shard_map/ppermute | solution.py:373
  10.5 2.5 %collective-permute-start.3 = (bf16[6,32,128]{2,1,0:T(8,128)(2,1)S(1)}, bf16[6,32,128]{2,1,0:T(8,128)(2,1)S(1)}, u32[]{:S(2)}, u32[]{:S(2)}) collective-permute-start(bf16[6,32,128]{2,1,0:T(8,128)(2,1)S(1)} %get-tuple-element.72), channel_id=1, source_target_pairs={{0,4},{1,5},{2,6},{3,7},{4,0},{5,1},{6,2},{7,3},{8,12},{9,13},{10,... | collective-permute-start | bytes 147464 | tf_op jit(solution)/shard_map/ppermute | solution.py:373
  10.5 2.5 %copy-start = (f32[4,8,32,128]{3,2,1,0:T(8,128)S(1)}, f32[4,8,32,128]{3,2,1,0:T(8,128)}, u32[]{:S(2)}) copy-start(f32[4,8,32,128]{3,2,1,0:T(8,128)} %param.7) | copy-start | bytes 1572868
  10.5 2.5 %copy-start.1 = (f32[4,8,32,128]{3,2,1,0:T(8,128)S(1)}, f32[4,8,32,128]{3,2,1,0:T(8,128)}, u32[]{:S(2)}) copy-start(f32[4,8,32,128]{3,2,1,0:T(8,128)} %param.6) | copy-start | bytes 1572868
  14.3 3.3 %collective-permute-start.5 = (bf16[12,32,128]{2,1,0:T(8,128)(2,1)S(1)}, bf16[12,32,128]{2,1,0:T(8,128)(2,1)S(1)}, u32[]{:S(2)}, u32[]{:S(2)}) collective-permute-start(bf16[12,32,128]{2,1,0:T(8,128)(2,1)S(1)} %get-tuple-element.80), channel_id=1, source_target_pairs={{0,4},{1,5},{2,6},{3,7},{4,0},{5,1},{6,2},{7,3},{8,12},{9,13},{10,... | collective-permute-start | bytes 294920 | tf_op jit(solution)/shard_map/ppermute | solution.py:373
  14.4 6.2 %collective-permute-start.4 = (bf16[12,32,128]{2,1,0:T(8,128)(2,1)S(1)}, bf16[12,32,128]{2,1,0:T(8,128)(2,1)S(1)}, u32[]{:S(2)}, u32[]{:S(2)}) collective-permute-start(bf16[12,32,128]{2,1,0:T(8,128)(2,1)S(1)} %get-tuple-element.79), channel_id=1, source_target_pairs={{0,1},{1,0},{2,3},{3,2},{4,8},{5,9},{6,10},{7,11},{8,4},{9,5},{10,... | collective-permute-start | bytes 294920 | tf_op jit(solution)/shard_map/ppermute | solution.py:373
  17.7 7.5 %collective-permute-start.6 = (bf16[16,32,128]{2,1,0:T(8,128)(2,1)S(1)}, bf16[16,32,128]{2,1,0:T(8,128)(2,1)S(1)}, u32[]{:S(2)}, u32[]{:S(2)}) collective-permute-start(bf16[16,32,128]{2,1,0:T(8,128)(2,1)S(1)} %get-tuple-element.81), channel_id=1, source_target_pairs={{0,1},{1,0},{2,3},{3,2},{4,5},{5,4},{6,7},{7,6},{8,9},{9,8},{10,11... | collective-permute-start | bytes 393224 | tf_op jit(solution)/shard_map/ppermute | solution.py:373
  18.3 6.9 %collective-permute-start.7 = (bf16[16,32,128]{2,1,0:T(8,128)(2,1)S(1)}, bf16[16,32,128]{2,1,0:T(8,128)(2,1)S(1)}, u32[]{:S(2)}, u32[]{:S(2)}) collective-permute-start(bf16[16,32,128]{2,1,0:T(8,128)(2,1)S(1)} %get-tuple-element.82), channel_id=1, source_target_pairs={{0,4},{1,2},{2,1},{3,7},{4,0},{5,6},{6,5},{7,3},{8,12},{9,10},{10,... | collective-permute-start | bytes 393224 | tf_op jit(solution)/shard_map/ppermute | solution.py:373
  20.7 4.0 %collective-permute-start.8 = (bf16[4,32,128]{2,1,0:T(8,128)(2,1)S(1)}, bf16[4,32,128]{2,1,0:T(8,128)(2,1)S(1)}, u32[]{:S(2)}, u32[]{:S(2)}) collective-permute-start(bf16[4,32,128]{2,1,0:T(8,128)(2,1)S(1)} %get-tuple-element.83), channel_id=1, source_target_pairs={{0,1},{1,0},{2,3},{3,2},{4,5},{5,4},{6,7},{7,6},{8,9},{9,8},{10,11... | collective-permute-start | bytes 98312 | tf_op jit(solution)/shard_map/ppermute | solution.py:373
  21.3 3.9 %collective-permute-start.9 = (bf16[4,32,128]{2,1,0:T(8,128)(2,1)S(1)}, bf16[4,32,128]{2,1,0:T(8,128)(2,1)S(1)}, u32[]{:S(2)}, u32[]{:S(2)}) collective-permute-start(bf16[4,32,128]{2,1,0:T(8,128)(2,1)S(1)} %get-tuple-element.84), channel_id=1, source_target_pairs={{0,4},{1,2},{2,1},{3,7},{4,0},{5,6},{6,5},{7,3},{8,12},{9,10},{10,... | collective-permute-start | bytes 98312 | tf_op jit(solution)/shard_map/ppermute | solution.py:373
  26.8 1.9 %collective-permute-start.11 = (bf16[12,32,128]{2,1,0:T(8,128)(2,1)S(1)}, bf16[12,32,128]{2,1,0:T(8,128)(2,1)S(1)}, u32[]{:S(2)}, u32[]{:S(2)}) collective-permute-start(bf16[12,32,128]{2,1,0:T(8,128)(2,1)S(1)} %get-tuple-element.88), channel_id=1, source_target_pairs={{0,4},{1,5},{2,6},{3,7},{4,0},{5,1},{6,2},{7,3},{8,12},{9,13},{10,... | collective-permute-start | bytes 294920 | tf_op jit(solution)/shard_map/ppermute | solution.py:373
  26.9 6.2 %collective-permute-start.10 = (bf16[12,32,128]{2,1,0:T(8,128)(2,1)S(1)}, bf16[12,32,128]{2,1,0:T(8,128)(2,1)S(1)}, u32[]{:S(2)}, u32[]{:S(2)}) collective-permute-start(bf16[12,32,128]{2,1,0:T(8,128)(2,1)S(1)} %get-tuple-element.87), channel_id=1, source_target_pairs={{0,1},{1,0},{2,3},{3,2},{4,8},{5,9},{6,10},{7,11},{8,4},{9,5},{10,... | collective-permute-start | bytes 294920 | tf_op jit(solution)/shard_map/ppermute | solution.py:373
  28.7 8.5 %collective-permute-start.12 = (bf16[16,32,128]{2,1,0:T(8,128)(2,1)S(1)}, bf16[16,32,128]{2,1,0:T(8,128)(2,1)S(1)}, u32[]{:S(2)}, u32[]{:S(2)}) collective-permute-start(bf16[16,32,128]{2,1,0:T(8,128)(2,1)S(1)} %get-tuple-element.89), channel_id=1, source_target_pairs={{0,1},{1,0},{2,3},{3,2},{4,5},{5,4},{6,7},{7,6},{8,9},{9,8},{10,11... | collective-permute-start | bytes 393224 | tf_op jit(solution)/shard_map/ppermute | solution.py:373
  29.0 8.2 %collective-permute-start.13 = (bf16[16,32,128]{2,1,0:T(8,128)(2,1)S(1)}, bf16[16,32,128]{2,1,0:T(8,128)(2,1)S(1)}, u32[]{:S(2)}, u32[]{:S(2)}) collective-permute-start(bf16[16,32,128]{2,1,0:T(8,128)(2,1)S(1)} %get-tuple-element.90), channel_id=1, source_target_pairs={{0,4},{1,2},{2,1},{3,7},{4,0},{5,6},{6,5},{7,3},{8,12},{9,10},{10,... | collective-permute-start | bytes 393224 | tf_op jit(solution)/shard_map/ppermute | solution.py:373
  33.1 4.0 %collective-permute-start.14 = (bf16[4,32,128]{2,1,0:T(8,128)(2,1)S(1)}, bf16[4,32,128]{2,1,0:T(8,128)(2,1)S(1)}, u32[]{:S(2)}, u32[]{:S(2)}) collective-permute-start(bf16[4,32,128]{2,1,0:T(8,128)(2,1)S(1)} %get-tuple-element.91), channel_id=1, source_target_pairs={{0,1},{1,0},{2,3},{3,2},{4,5},{5,4},{6,7},{7,6},{8,9},{9,8},{10,11... | collective-permute-start | bytes 98312 | tf_op jit(solution)/shard_map/ppermute | solution.py:373
  33.2 3.9 %collective-permute-start.15 = (bf16[4,32,128]{2,1,0:T(8,128)(2,1)S(1)}, bf16[4,32,128]{2,1,0:T(8,128)(2,1)S(1)}, u32[]{:S(2)}, u32[]{:S(2)}) collective-permute-start(bf16[4,32,128]{2,1,0:T(8,128)(2,1)S(1)} %get-tuple-element.92), channel_id=1, source_target_pairs={{0,4},{1,2},{2,1},{3,7},{4,0},{5,6},{6,5},{7,3},{8,12},{9,10},{10,... | collective-permute-start | bytes 98312 | tf_op jit(solution)/shard_map/ppermute | solution.py:373
  38.9 1.4 %collective-permute-start.17 = (bf16[12,32,128]{2,1,0:T(8,128)(2,1)S(1)}, bf16[12,32,128]{2,1,0:T(8,128)(2,1)S(1)}, u32[]{:S(2)}, u32[]{:S(2)}) collective-permute-start(bf16[12,32,128]{2,1,0:T(8,128)(2,1)S(1)} %get-tuple-element.96), channel_id=1, source_target_pairs={{0,4},{1,5},{2,6},{3,7},{4,0},{5,1},{6,2},{7,3},{8,12},{9,13},{10,... | collective-permute-start | bytes 294920 | tf_op jit(solution)/shard_map/ppermute | solution.py:373
  39.0 6.2 %collective-permute-start.16 = (bf16[12,32,128]{2,1,0:T(8,128)(2,1)S(1)}, bf16[12,32,128]{2,1,0:T(8,128)(2,1)S(1)}, u32[]{:S(2)}, u32[]{:S(2)}) collective-permute-start(bf16[12,32,128]{2,1,0:T(8,128)(2,1)S(1)} %get-tuple-element.95), channel_id=1, source_target_pairs={{0,1},{1,0},{2,3},{3,2},{4,8},{5,9},{6,10},{7,11},{8,4},{9,5},{10,... | collective-permute-start | bytes 294920 | tf_op jit(solution)/shard_map/ppermute | solution.py:373
  40.4 9.0 %collective-permute-start.18 = (bf16[16,32,128]{2,1,0:T(8,128)(2,1)S(1)}, bf16[16,32,128]{2,1,0:T(8,128)(2,1)S(1)}, u32[]{:S(2)}, u32[]{:S(2)}) collective-permute-start(bf16[16,32,128]{2,1,0:T(8,128)(2,1)S(1)} %get-tuple-element.97), channel_id=1, source_target_pairs={{0,1},{1,0},{2,3},{3,2},{4,5},{5,4},{6,7},{7,6},{8,9},{9,8},{10,11... | collective-permute-start | bytes 393224 | tf_op jit(solution)/shard_map/ppermute | solution.py:373
  40.5 8.9 %collective-permute-start.19 = (bf16[16,32,128]{2,1,0:T(8,128)(2,1)S(1)}, bf16[16,32,128]{2,1,0:T(8,128)(2,1)S(1)}, u32[]{:S(2)}, u32[]{:S(2)}) collective-permute-start(bf16[16,32,128]{2,1,0:T(8,128)(2,1)S(1)} %get-tuple-element.98), channel_id=1, source_target_pairs={{0,4},{1,2},{2,1},{3,7},{4,0},{5,6},{6,5},{7,3},{8,12},{9,10},{10,... | collective-permute-start | bytes 393224 | tf_op jit(solution)/shard_map/ppermute | solution.py:373
  45.3 4.0 %collective-permute-start.20 = (bf16[4,32,128]{2,1,0:T(8,128)(2,1)S(1)}, bf16[4,32,128]{2,1,0:T(8,128)(2,1)S(1)}, u32[]{:S(2)}, u32[]{:S(2)}) collective-permute-start(bf16[4,32,128]{2,1,0:T(8,128)(2,1)S(1)} %get-tuple-element.99), channel_id=1, source_target_pairs={{0,1},{1,0},{2,3},{3,2},{4,5},{5,4},{6,7},{7,6},{8,9},{9,8},{10,11... | collective-permute-start | bytes 98312 | tf_op jit(solution)/shard_map/ppermute | solution.py:373
  45.4 4.0 %collective-permute-start.21 = (bf16[4,32,128]{2,1,0:T(8,128)(2,1)S(1)}, bf16[4,32,128]{2,1,0:T(8,128)(2,1)S(1)}, u32[]{:S(2)}, u32[]{:S(2)}) collective-permute-start(bf16[4,32,128]{2,1,0:T(8,128)(2,1)S(1)} %get-tuple-element.100), channel_id=1, source_target_pairs={{0,4},{1,2},{2,1},{3,7},{4,0},{5,6},{6,5},{7,3},{8,12},{9,10},{10,... | collective-permute-start | bytes 98312 | tf_op jit(solution)/shard_map/ppermute | solution.py:373
  50.9 1.4 %collective-permute-start.23 = (bf16[12,32,128]{2,1,0:T(8,128)(2,1)S(1)}, bf16[12,32,128]{2,1,0:T(8,128)(2,1)S(1)}, u32[]{:S(2)}, u32[]{:S(2)}) collective-permute-start(bf16[12,32,128]{2,1,0:T(8,128)(2,1)S(1)} %get-tuple-element.104), channel_id=1, source_target_pairs={{0,4},{1,5},{2,6},{3,7},{4,0},{5,1},{6,2},{7,3},{8,12},{9,13},{10,... | collective-permute-start | bytes 294920 | tf_op jit(solution)/shard_map/ppermute | solution.py:373
  51.0 6.2 %collective-permute-start.22 = (bf16[12,32,128]{2,1,0:T(8,128)(2,1)S(1)}, bf16[12,32,128]{2,1,0:T(8,128)(2,1)S(1)}, u32[]{:S(2)}, u32[]{:S(2)}) collective-permute-start(bf16[12,32,128]{2,1,0:T(8,128)(2,1)S(1)} %get-tuple-element.103), channel_id=1, source_target_pairs={{0,1},{1,0},{2,3},{3,2},{4,8},{5,9},{6,10},{7,11},{8,4},{9,5},{10,... | collective-permute-start | bytes 294920 | tf_op jit(solution)/shard_map/ppermute | solution.py:373
  52.4 9.0 %collective-permute-start.24 = (bf16[16,32,128]{2,1,0:T(8,128)(2,1)S(1)}, bf16[16,32,128]{2,1,0:T(8,128)(2,1)S(1)}, u32[]{:S(2)}, u32[]{:S(2)}) collective-permute-start(bf16[16,32,128]{2,1,0:T(8,128)(2,1)S(1)} %get-tuple-element.105), channel_id=1, source_target_pairs={{0,1},{1,0},{2,3},{3,2},{4,5},{5,4},{6,7},{7,6},{8,9},{9,8},{10,11... | collective-permute-start | bytes 393224 | tf_op jit(solution)/shard_map/ppermute | solution.py:373
  52.5 8.9 %collective-permute-start.25 = (bf16[16,32,128]{2,1,0:T(8,128)(2,1)S(1)}, bf16[16,32,128]{2,1,0:T(8,128)(2,1)S(1)}, u32[]{:S(2)}, u32[]{:S(2)}) collective-permute-start(bf16[16,32,128]{2,1,0:T(8,128)(2,1)S(1)} %get-tuple-element.106), channel_id=1, source_target_pairs={{0,4},{1,2},{2,1},{3,7},{4,0},{5,6},{6,5},{7,3},{8,12},{9,10},{10,... | collective-permute-start | bytes 393224 | tf_op jit(solution)/shard_map/ppermute | solution.py:373
  57.3 4.0 %collective-permute-start.26 = (bf16[4,32,128]{2,1,0:T(8,128)(2,1)S(1)}, bf16[4,32,128]{2,1,0:T(8,128)(2,1)S(1)}, u32[]{:S(2)}, u32[]{:S(2)}) collective-permute-start(bf16[4,32,128]{2,1,0:T(8,128)(2,1)S(1)} %get-tuple-element.107), channel_id=1, source_target_pairs={{0,1},{1,0},{2,3},{3,2},{4,5},{5,4},{6,7},{7,6},{8,9},{9,8},{10,11... | collective-permute-start | bytes 98312 | tf_op jit(solution)/shard_map/ppermute | solution.py:373
  57.4 4.0 %collective-permute-start.27 = (bf16[4,32,128]{2,1,0:T(8,128)(2,1)S(1)}, bf16[4,32,128]{2,1,0:T(8,128)(2,1)S(1)}, u32[]{:S(2)}, u32[]{:S(2)}) collective-permute-start(bf16[4,32,128]{2,1,0:T(8,128)(2,1)S(1)} %get-tuple-element.108), channel_id=1, source_target_pairs={{0,4},{1,2},{2,1},{3,7},{4,0},{5,6},{6,5},{7,3},{8,12},{9,10},{10,... | collective-permute-start | bytes 98312 | tf_op jit(solution)/shard_map/ppermute | solution.py:373
  62.9 5.7 %collective-permute-start.28 = (bf16[6,32,128]{2,1,0:T(8,128)(2,1)S(1)}, bf16[6,32,128]{2,1,0:T(8,128)(2,1)S(1)}, u32[]{:S(2)}, u32[]{:S(2)}) collective-permute-start(bf16[6,32,128]{2,1,0:T(8,128)(2,1)S(1)} %get-tuple-element.111), channel_id=1, source_target_pairs={{0,1},{1,0},{2,3},{3,2},{4,8},{5,9},{6,10},{7,11},{8,4},{9,5},{10,... | collective-permute-start | bytes 147464 | tf_op jit(solution)/shard_map/ppermute | solution.py:373
  63.0 5.6 %collective-permute-start.29 = (bf16[6,32,128]{2,1,0:T(8,128)(2,1)S(1)}, bf16[6,32,128]{2,1,0:T(8,128)(2,1)S(1)}, u32[]{:S(2)}, u32[]{:S(2)}) collective-permute-start(bf16[6,32,128]{2,1,0:T(8,128)(2,1)S(1)} %get-tuple-element.112), channel_id=1, source_target_pairs={{0,4},{1,5},{2,6},{3,7},{4,0},{5,1},{6,2},{7,3},{8,12},{9,13},{10,... | collective-permute-start | bytes 147464 | tf_op jit(solution)/shard_map/ppermute | solution.py:373
  68.7 4.3 %collective-permute-start.30 = (bf16[8,32,128]{2,1,0:T(8,128)(2,1)S(1)}, bf16[8,32,128]{2,1,0:T(8,128)(2,1)S(1)}, u32[]{:S(2)}, u32[]{:S(2)}) collective-permute-start(bf16[8,32,128]{2,1,0:T(8,128)(2,1)S(1)} %get-tuple-element.113), channel_id=1, source_target_pairs={{0,1},{1,0},{2,3},{3,2},{4,5},{5,4},{6,7},{7,6},{8,9},{9,8},{10,11... | collective-permute-start | bytes 196616 | tf_op jit(solution)/shard_map/ppermute | solution.py:373
  68.8 4.3 %collective-permute-start.31 = (bf16[8,32,128]{2,1,0:T(8,128)(2,1)S(1)}, bf16[8,32,128]{2,1,0:T(8,128)(2,1)S(1)}, u32[]{:S(2)}, u32[]{:S(2)}) collective-permute-start(bf16[8,32,128]{2,1,0:T(8,128)(2,1)S(1)} %get-tuple-element.114), channel_id=1, source_target_pairs={{0,4},{1,2},{2,1},{3,7},{4,0},{5,6},{6,5},{7,3},{8,12},{9,10},{10,... | collective-permute-start | bytes 196616 | tf_op jit(solution)/shard_map/ppermute | solution.py:373
where the time goes:
time: 74.4 us; the launch traced here: 74 us
  starting transfers between devices  29.8 us (40%)
  waiting for transfers between devices  27.1 us (36%)
  Pallas kernels  12.5 us (17%)
  local copies, waits for them, and re-layouts  2.82 us (4%)
  between operations  1.71 us (2%)
    ppermute x32, starting transfers between devices, send(): return lax.ppermute(value, ('wide', 'narrow'), ring)  29.8 us
    ppermute x32, waiting for transfers between devices, send(): return lax.ppermute(value, ('wide', 'narrow'), ring)  27.1 us
    pallas_call x14, Pallas kernels, call(): pl.pallas_call(kernel, out_shape=outputs, in_specs=[smem] * scalars + [vm...  7.99 us
    pallas_call x1, Pallas kernels, local(): pl.pallas_call(turn_kernel, out_shape=[half_shape] * 4, in_specs=[smem, p...  1.96 us
    pallas_call x2, Pallas kernels, final_call(): pl.pallas_call(functools.partial(final_kernel, sizes, rows), out_shape=ja...  1.5 us
  transfers between devices with their start and end apart: 32, of which 18 were waited for; matrix products, arithmetic and copies ran while one was open for 2% of the time, Pallas kernels for 5%

commit v1 on v0

--- a/solution.py
+++ b/solution.py
@@ -297,25 +297,45 @@
                 out_ref[step * 2 + place] = cast_low(value)
 
 
-def last_kernel(sizes, info_ref, grad_in, next_in, pair_in, near_ref, far_ref):
-    tile_x, tile_y, _ = sizes
-    span = tile_y + 2
-    even = info_ref[ROW_EVEN] == 1
-    for out_ref, lower in ((near_ref, even), (far_ref, jnp.logical_not(even))):
+def last_inner_kernel(sizes, info_ref, grad_in, pair_in, near_ref, far_ref):
+    tile_x, tile_y, _ = sizes
+    span = tile_y + 2
+    even = info_ref[EVEN] == 1
+    row_even = info_ref[ROW_EVEN] == 1
+    first = jnp.where(even, 2, 1)
+    for out_ref, lower in ((near_ref, row_even), (far_ref, jnp.logical_not(row_even))):
         row = jnp.where(lower, tile_x + 1, 0)
-        for col in range(1, tile_y + 1):
-            value = grad_in[row * span + col]
-            came = came_along_wide(sizes, True, info_ref, pair_in, next_in, row, col)
-            out_ref[col - 1] = cast_low(value if came is None else value + came)
+        came = wide_value(pair_in[row])
+        for place in range(tile_y - 1):
+            value = grad_in[row * span + first + place]
+            if place == 0:
+                value = value + kept(came, even)
+            if place == tile_y - 2:
+                value = value + kept(came, jnp.logical_not(even))
+            out_ref[place] = cast_low(value)
+
+
+def last_ends_kernel(sizes, info_ref, grad_in, next_in, near_ref, far_ref):
+    tile_x, tile_y, _ = sizes
+    span = tile_y + 2
+    even = info_ref[EVEN] == 1
+    row_even = info_ref[ROW_EVEN] == 1
+    col = jnp.where(even, 1, tile_y)
+    nobody = jnp.where(even, info_ref[COL_FIRST], info_ref[COL_LAST]) == 1
+    for out_ref, lower in ((near_ref, row_even), (far_ref, jnp.logical_not(row_even))):
+        row = jnp.where(lower, tile_x + 1, 0)
+        came = wide_value(kept(next_in[row], nobody))
+        out_ref[0] = cast_low(grad_in[row * span + col] + came)
 
 
 def final_kernel(sizes, rows, info_ref, x_in, grad_in, next_in, pair_in, *rest):
     tile_x, tile_y, _ = sizes
     span = tile_y + 2
     if len(rest) > 3:
-        near_in, far_in, _, out_ref, part_ref, sent = rest
+        near_in, far_in, near_end, far_end, _, out_ref, part_ref, sent = rest
     else:
         out_ref, part_ref, sent = rest
+    even = info_ref[EVEN] == 1
     copies = []
     for place, row in enumerate(rows):
         for col in range(1, tile_y + 1):
@@ -324,10 +344,16 @@
             came = came_along_wide(sizes, True, info_ref, pair_in, next_in, row, col)
             if came is not None:
                 gradient = gradient + came
-            if row == 1:
-                gradient = gradient + came_along_narrow(info_ref, near_in, far_in, True, col - 1)
-            if row == tile_x:
-                gradient = gradient + came_along_narrow(info_ref, near_in, far_in, False, col - 1)
+            for edge in (1, tile_x):
+                if row != edge:
+                    continue
+                upper = edge == 1
+                inner = jnp.where(even, jnp.maximum(col - 2, 0), jnp.minimum(col - 1, tile_y - 2))
+                came = came_along_narrow(info_ref, near_in, far_in, upper, inner)
+                if col in (1, tile_y):
+                    end = came_along_narrow(info_ref, near_end, far_end, upper, 0)
+                    came = jnp.where(even if col == 1 else jnp.logical_not(even), end, came)
+                gradient = gradient + came
             part_ref[place, col - 1] = x_in[at] - descent * gradient
         copies.append(pltpu.make_async_copy(part_ref.at[place], out_ref.at[row - 1], sent.at[place]))
         copies[-1].start()
@@ -479,7 +505,10 @@
         last = iteration == ITERS - 1
         next_in, pair_in = along_wide(next_out, pair_out)
         if last:
-            folds = [(last_kernel, "rows_beyond", [next_in, pair_in], tile_y)]
+            folds = [
+                (last_inner_kernel, "inner_beyond", [pair_in], tile_y - 1),
+                (last_ends_kernel, "end_beyond", [next_in], 1),
+            ]
         else:
             folds = [
                 (inner_kernel, "inner_columns", [pair_in], 2 * (span - 2)),
@@ -521,7 +550,7 @@
                 )(*operands)
 
             started = final_call(inner, inputs, {}, "inner_rows")
-            updated = final_call(outer, inputs + [*came, started], {7: 0}, "outer_rows")
+            updated = final_call(outer, inputs + [*came, started], {9: 0}, "outer_rows")
         else:
             ending = iteration == ITERS - 2
             x, grad, next_out, pair_out, *rest = call(

time: 74.4 us -> 73.8 us (level)
  starting transfers between devices: 29.8 us -> 28.6 us
    ppermute x32 -> x34, starting transfers between devices: 29.8 us -> 28.6 us  [send(): return lax.ppermute(value, ('wide', 'narrow'), ring)]
    ppermute x32 -> x34, waiting for transfers between devices: 27.1 us -> 27.7 us  [send(): return lax.ppermute(value, ('wide', 'narrow'), ring)]
    pallas_call x14 -> x15, Pallas kernels: 7.99 us -> 8.24 us  [call(): pl.pallas_call(kernel, out_shape=outputs, in_specs=[smem] * scalars + [vm...]
  transfers between devices with their start and end apart: 32 -> 34, of which waited for: 18 -> 19; matrix products, arithmetic and copies ran while one was open for 2% -> 2% of each run, Pallas kernels for 5% -> 5%
where the time goes in v1:
time: 73.8 us; the launch traced here: 73.7 us
  starting transfers between devices  28.6 us (39%)
  waiting for transfers between devices  27.7 us (38%)
  Pallas kernels  12.8 us (17%)
  local copies, waits for them, and re-layouts  2.82 us (4%)
  between operations  1.77 us (2%)
    ppermute x34, starting transfers between devices, send(): return lax.ppermute(value, ('wide', 'narrow'), ring)  28.6 us
    ppermute x34, waiting for transfers between devices, send(): return lax.ppermute(value, ('wide', 'narrow'), ring)  27.7 us
    pallas_call x15, Pallas kernels, call(): pl.pallas_call(kernel, out_shape=outputs, in_specs=[smem] * scalars + [vm...  8.24 us
    pallas_call x1, Pallas kernels, local(): pl.pallas_call(turn_kernel, out_shape=[half_shape] * 4, in_specs=[smem, p...  1.96 us
    pallas_call x2, Pallas kernels, final_call(): pl.pallas_call(functools.partial(final_kernel, sizes, rows), out_shape=ja...  1.51 us
  transfers between devices with their start and end apart: 34, of which 19 were waited for; matrix products, arithmetic and copies ran while one was open for 2% of the time, Pallas kernels for 5%

profile of v1, /device:TPU:26, one launch (start us, length us, event | category | flops | bytes accessed | tf_op | source)
XLA Modules:
  0.0 73.7 jit_solution(2589701028603644428)
XLA Ops:
  0.6 1.0 %slice_bitcast_fusion = (bf16[8,32,128]{2,1,0:T(8,128)(2,1)S(1)}, bf16[8,32,128]{2,1,0:T(8,128)(2,1)S(1)}) fusion(f32[4,8,32,128]{3,2,1,0:T(8,128)} %param.6), kind=kLoop, calls=%fused_computation.2 | loop fusion | bytes 262144 | tf_op jit(solution)/shard_map/squeeze | solution.py:447
  1.7 0.6 collective-permute-start
  2.3 2.2 %collective-permute-start.1 = (bf16[8,32,128]{2,1,0:T(8,128)(2,1)S(1)}, bf16[8,32,128]{2,1,0:T(8,128)(2,1)S(1)}, u32[]{:S(2)}, u32[]{:S(2)}) collective-permute-start(bf16[8,32,128]{2,1,0:T(8,128)(2,1)S(1)} %get-tuple-element.64), channel_id=1, source_target_pairs={{0,4},{1,2},{2,1},{3,7},{4,0},{5,6},{6,5},{7,3},{8,12},{9,10},{10,... | collective-permute-start | bytes 196616 | tf_op jit(solution)/shard_map/ppermute | solution.py:399
  4.4 0.9 %slice_bitcast_fusion.2 = (bf16[4,32,128]{2,1,0:T(8,128)(2,1)S(1)}, bf16[4,32,128]{2,1,0:T(8,128)(2,1)S(1)}) fusion(f32[4,8,32,128]{3,2,1,0:T(8,128)} %param.6), kind=kLoop, calls=%fused_computation.4 | loop fusion | bytes 131072 | tf_op jit(solution)/shard_map/squeeze | solution.py:486
  6.0 0.1 stack.27
  6.1 1.1 %plan_slots.1 = (s32[7]{0:T(128)S(4)}, s32[128]{0:T(128)S(4)}, s32[128]{0:T(128)S(4)}) custom-call(s32[6]{0:T(128)S(1)} %convert_element_type.17.flags_ref, s32[1,1]{1,0:T(1,128)S(6)} %copy.14.live_ref, s32[128]{0:T(128)} %bitcast.32, s32[128]{0:T(128)} %bitcast.33), custom_call_target="tpu_custom_call" | custom-call | flops 268435456 | bytes 1048576 | tf_op jit(solution)/shard_map/plan_slots/pallas_call | solution.py:453
  7.3 3.2 %collective-permute-start.2 = (bf16[6,32,128]{2,1,0:T(8,128)(2,1)S(1)}, bf16[6,32,128]{2,1,0:T(8,128)(2,1)S(1)}, u32[]{:S(2)}, u32[]{:S(2)}) collective-permute-start(bf16[6,32,128]{2,1,0:T(8,128)(2,1)S(1)} %get-tuple-element.73), channel_id=1, source_target_pairs={{0,1},{1,0},{2,3},{3,2},{4,8},{5,9},{6,10},{7,11},{8,4},{9,5},{10,... | collective-permute-start | bytes 147464 | tf_op jit(solution)/shard_map/ppermute | solution.py:399
  10.5 2.0 %turn_blocks.1 = (bf16[64,128,128]{2,1,0:T(8,128)(2,1)S(1)}, bf16[64,128,128]{2,1,0:T(8,128)(2,1)S(1)}, bf16[64,128,128]{2,1,0:T(8,128)(2,1)S(1)}, bf16[64,128,128]{2,1,0:T(8,128)(2,1)S(1)}) custom-call(s32[7]{0:T(128)S(4)} %get-tuple-element.66.info_ref, bf16[128,128,128]{2,1,0:T(8,128)(2,1)} %bitcast.30), custom_call_target="tpu_custom_call" | custom-call | flops 268435456 | bytes 4194304 | tf_op jit(solution)/shard_map/turn_blocks/pallas_call | solution.py:473
  12.4 0.6 collective-permute-done.2.next_in
  13.0 1.4 %first_step.1 = (f32[60,32,128]{2,1,0:T(8,128)S(1)}, f32[61,32,128]{2,1,0:T(8,128)S(1)}, bf16[12,32,128]{2,1,0:T(8,128)(2,1)S(1)}, bf16[12,32,128]{2,1,0:T(8,128)(2,1)S(1)}) custom-call(s32[7]{0:T(128)S(4)} %get-tuple-element.66.info_ref, s32[128]{0:T(128)S(4)} %get-tuple-element.67.rows_ref, s32[128]{0:T(128)S(4)} %get-tuple-element.68.cols_ref, ...), custom_call_target="tpu_custom_call" | custom-call | flops 268435456 | bytes 1048576 | tf_op jit(solution)/shard_map/first_step/pallas_call | solution.py:419
  14.5 3.2 %collective-permute-start.4 = (bf16[12,32,128]{2,1,0:T(8,128)(2,1)S(1)}, bf16[12,32,128]{2,1,0:T(8,128)(2,1)S(1)}, u32[]{:S(2)}, u32[]{:S(2)}) collective-permute-start(bf16[12,32,128]{2,1,0:T(8,128)(2,1)S(1)} %get-tuple-element.81), channel_id=1, source_target_pairs={{0,1},{1,0},{2,3},{3,2},{4,8},{5,9},{6,10},{7,11},{8,4},{9,5},{10,... | collective-permute-start | bytes 294920 | tf_op jit(solution)/shard_map/ppermute | solution.py:399
  17.7 0.6 collective-permute-start.6
  18.3 1.5 %collective-permute-start.7 = (bf16[16,32,128]{2,1,0:T(8,128)(2,1)S(1)}, bf16[16,32,128]{2,1,0:T(8,128)(2,1)S(1)}, u32[]{:S(2)}, u32[]{:S(2)}) collective-permute-start(bf16[16,32,128]{2,1,0:T(8,128)(2,1)S(1)} %get-tuple-element.84), channel_id=1, source_target_pairs={{0,4},{1,2},{2,1},{3,7},{4,0},{5,6},{6,5},{7,3},{8,12},{9,10},{10,... | collective-permute-start | bytes 393224 | tf_op jit(solution)/shard_map/ppermute | solution.py:399
  19.9 0.8 %collective-permute-done.4.next_in = bf16[12,32,128]{2,1,0:T(8,128)(2,1)S(1)} collective-permute-done((bf16[12,32,128]{2,1,0:T(8,128)(2,1)S(1)}, bf16[12,32,128]{2,1,0:T(8,128)(2,1)S(1)}, u32[]{:S(2)}, u32[]{:S(2)}) %collective-permute-start.4) | collective-permute-done | bytes 98336 | tf_op jit(solution)/shard_map/ppermute | solution.py:399
  20.7 0.6 collective-permute-start.8
  21.3 1.5 %collective-permute-start.9 = (bf16[4,32,128]{2,1,0:T(8,128)(2,1)S(1)}, bf16[4,32,128]{2,1,0:T(8,128)(2,1)S(1)}, u32[]{:S(2)}, u32[]{:S(2)}) collective-permute-start(bf16[4,32,128]{2,1,0:T(8,128)(2,1)S(1)} %get-tuple-element.86), channel_id=1, source_target_pairs={{0,4},{1,2},{2,1},{3,7},{4,0},{5,6},{6,5},{7,3},{8,12},{9,10},{10,... | collective-permute-start | bytes 98312 | tf_op jit(solution)/shard_map/ppermute | solution.py:399
  22.8 2.0 %collective-permute-done.8.near_ends = bf16[4,32,128]{2,1,0:T(8,128)(2,1)S(1)} collective-permute-done((bf16[4,32,128]{2,1,0:T(8,128)(2,1)S(1)}, bf16[4,32,128]{2,1,0:T(8,128)(2,1)S(1)}, u32[]{:S(2)}, u32[]{:S(2)}) %collective-permute-start.8) | collective-permute-done | bytes 32800 | tf_op jit(solution)/shard_map/ppermute | solution.py:399
  24.7 0.5 collective-permute-done.9.far_ends
  25.2 1.6 %one_step.4 = (f32[60,32,128]{2,1,0:T(8,128)S(1)}, f32[61,32,128]{2,1,0:T(8,128)S(1)}, bf16[12,32,128]{2,1,0:T(8,128)(2,1)S(1)}, bf16[12,32,128]{2,1,0:T(8,128)(2,1)S(1)}) custom-call(s32[7]{0:T(128)S(4)} %get-tuple-element.66.info_ref, s32[128]{0:T(128)S(4)} %get-tuple-element.67.rows_ref, s32[128]{0:T(128)S(4)} %get-tuple-element.68.cols_ref, ...), custom_call_target="tpu_custom_call" | custom-call | flops 268435456 | bytes 1048576 | tf_op jit(solution)/shard_map/one_step/pallas_call | solution.py:419
  26.9 1.8 %collective-permute-start.10 = (bf16[12,32,128]{2,1,0:T(8,128)(2,1)S(1)}, bf16[12,32,128]{2,1,0:T(8,128)(2,1)S(1)}, u32[]{:S(2)}, u32[]{:S(2)}) collective-permute-start(bf16[12,32,128]{2,1,0:T(8,128)(2,1)S(1)} %get-tuple-element.89), channel_id=1, source_target_pairs={{0,1},{1,0},{2,3},{3,2},{4,8},{5,9},{6,10},{7,11},{8,4},{9,5},{10,... | collective-permute-start | bytes 294920 | tf_op jit(solution)/shard_map/ppermute | solution.py:399
  28.8 0.3 collective-permute-start.12
  29.1 1.6 %collective-permute-start.13 = (bf16[16,32,128]{2,1,0:T(8,128)(2,1)S(1)}, bf16[16,32,128]{2,1,0:T(8,128)(2,1)S(1)}, u32[]{:S(2)}, u32[]{:S(2)}) collective-permute-start(bf16[16,32,128]{2,1,0:T(8,128)(2,1)S(1)} %get-tuple-element.92), channel_id=1, source_target_pairs={{0,4},{1,2},{2,1},{3,7},{4,0},{5,6},{6,5},{7,3},{8,12},{9,10},{10,... | collective-permute-start | bytes 393224 | tf_op jit(solution)/shard_map/ppermute | solution.py:399
  30.7 2.5 %collective-permute-done.10.next_in = bf16[12,32,128]{2,1,0:T(8,128)(2,1)S(1)} collective-permute-done((bf16[12,32,128]{2,1,0:T(8,128)(2,1)S(1)}, bf16[12,32,128]{2,1,0:T(8,128)(2,1)S(1)}, u32[]{:S(2)}, u32[]{:S(2)}) %collective-permute-start.10) | collective-permute-done | bytes 98336 | tf_op jit(solution)/shard_map/ppermute | solution.py:399
  33.3 1.5 %collective-permute-start.15 = (bf16[4,32,128]{2,1,0:T(8,128)(2,1)S(1)}, bf16[4,32,128]{2,1,0:T(8,128)(2,1)S(1)}, u32[]{:S(2)}, u32[]{:S(2)}) collective-permute-start(bf16[4,32,128]{2,1,0:T(8,128)(2,1)S(1)} %get-tuple-element.94), channel_id=1, source_target_pairs={{0,4},{1,2},{2,1},{3,7},{4,0},{5,6},{6,5},{7,3},{8,12},{9,10},{10,... | collective-permute-start | bytes 98312 | tf_op jit(solution)/shard_map/ppermute | solution.py:399
  34.8 2.4 %collective-permute-done.14.near_ends = bf16[4,32,128]{2,1,0:T(8,128)(2,1)S(1)} collective-permute-done((bf16[4,32,128]{2,1,0:T(8,128)(2,1)S(1)}, bf16[4,32,128]{2,1,0:T(8,128)(2,1)S(1)}, u32[]{:S(2)}, u32[]{:S(2)}) %collective-permute-start.14) | collective-permute-done | bytes 32800 | tf_op jit(solution)/shard_map/ppermute | solution.py:399
  37.2 0.1 collective-permute-done.15.far_ends
  37.3 1.8 %one_step.5 = (f32[60,32,128]{2,1,0:T(8,128)S(1)}, f32[61,32,128]{2,1,0:T(8,128)S(1)}, bf16[12,32,128]{2,1,0:T(8,128)(2,1)S(1)}, bf16[12,32,128]{2,1,0:T(8,128)(2,1)S(1)}) custom-call(s32[7]{0:T(128)S(4)} %get-tuple-element.66.info_ref, s32[128]{0:T(128)S(4)} %get-tuple-element.67.rows_ref, s32[128]{0:T(128)S(4)} %get-tuple-element.68.cols_ref, ...), custom_call_target="tpu_custom_call" | custom-call | flops 268435456 | bytes 1048576 | tf_op jit(solution)/shard_map/one_step/pallas_call | solution.py:419
  39.1 0.7 collective-permute-start.16
  39.9 0.6 collective-permute-done.17.pair_in
  40.6 1.4 %collective-permute-start.19 = (bf16[16,32,128]{2,1,0:T(8,128)(2,1)S(1)}, bf16[16,32,128]{2,1,0:T(8,128)(2,1)S(1)}, u32[]{:S(2)}, u32[]{:S(2)}) collective-permute-start(bf16[16,32,128]{2,1,0:T(8,128)(2,1)S(1)} %get-tuple-element.100), channel_id=1, source_target_pairs={{0,4},{1,2},{2,1},{3,7},{4,0},{5,6},{6,5},{7,3},{8,12},{9,10},{10,... | collective-permute-start | bytes 393224 | tf_op jit(solution)/shard_map/ppermute | solution.py:399
  42.0 3.4 %collective-permute-done.16.next_in = bf16[12,32,128]{2,1,0:T(8,128)(2,1)S(1)} collective-permute-done((bf16[12,32,128]{2,1,0:T(8,128)(2,1)S(1)}, bf16[12,32,128]{2,1,0:T(8,128)(2,1)S(1)}, u32[]{:S(2)}, u32[]{:S(2)}) %collective-permute-start.16) | collective-permute-done | bytes 98336 | tf_op jit(solution)/shard_map/ppermute | solution.py:399
  45.5 1.4 %collective-permute-start.21 = (bf16[4,32,128]{2,1,0:T(8,128)(2,1)S(1)}, bf16[4,32,128]{2,1,0:T(8,128)(2,1)S(1)}, u32[]{:S(2)}, u32[]{:S(2)}) collective-permute-start(bf16[4,32,128]{2,1,0:T(8,128)(2,1)S(1)} %get-tuple-element.102), channel_id=1, source_target_pairs={{0,4},{1,2},{2,1},{3,7},{4,0},{5,6},{6,5},{7,3},{8,12},{9,10},{10,... | collective-permute-start | bytes 98312 | tf_op jit(solution)/shard_map/ppermute | solution.py:399
  46.9 2.5 %collective-permute-done.20.near_ends = bf16[4,32,128]{2,1,0:T(8,128)(2,1)S(1)} collective-permute-done((bf16[4,32,128]{2,1,0:T(8,128)(2,1)S(1)}, bf16[4,32,128]{2,1,0:T(8,128)(2,1)S(1)}, u32[]{:S(2)}, u32[]{:S(2)}) %collective-permute-start.20) | collective-permute-done | bytes 32800 | tf_op jit(solution)/shard_map/ppermute | solution.py:399
  49.5 1.6 %one_step.6 = (f32[60,32,128]{2,1,0:T(8,128)S(1)}, f32[61,32,128]{2,1,0:T(8,128)S(1)}, bf16[12,32,128]{2,1,0:T(8,128)(2,1)S(1)}, bf16[12,32,128]{2,1,0:T(8,128)(2,1)S(1)}) custom-call(s32[7]{0:T(128)S(4)} %get-tuple-element.66.info_ref, s32[128]{0:T(128)S(4)} %get-tuple-element.67.rows_ref, s32[128]{0:T(128)S(4)} %get-tuple-element.68.cols_ref, ...), custom_call_target="tpu_custom_call" | custom-call | flops 268435456 | bytes 1048576 | tf_op jit(solution)/shard_map/one_step/pallas_call | solution.py:419
  51.3 1.2 %collective-permute-done.23.pair_in = bf16[12,32,128]{2,1,0:T(8,128)(2,1)S(1)} collective-permute-done((bf16[12,32,128]{2,1,0:T(8,128)(2,1)S(1)}, bf16[12,32,128]{2,1,0:T(8,128)(2,1)S(1)}, u32[]{:S(2)}, u32[]{:S(2)}) %collective-permute-start.23) | collective-permute-done | bytes 98336 | tf_op jit(solution)/shard_map/ppermute | solution.py:399
  52.6 1.4 %collective-permute-start.25 = (bf16[16,32,128]{2,1,0:T(8,128)(2,1)S(1)}, bf16[16,32,128]{2,1,0:T(8,128)(2,1)S(1)}, u32[]{:S(2)}, u32[]{:S(2)}) collective-permute-start(bf16[16,32,128]{2,1,0:T(8,128)(2,1)S(1)} %get-tuple-element.108), channel_id=1, source_target_pairs={{0,4},{1,2},{2,1},{3,7},{4,0},{5,6},{6,5},{7,3},{8,12},{9,10},{10,... | collective-permute-start | bytes 393224 | tf_op jit(solution)/shard_map/ppermute | solution.py:399
  54.0 3.4 %collective-permute-done.22.next_in = bf16[12,32,128]{2,1,0:T(8,128)(2,1)S(1)} collective-permute-done((bf16[12,32,128]{2,1,0:T(8,128)(2,1)S(1)}, bf16[12,32,128]{2,1,0:T(8,128)(2,1)S(1)}, u32[]{:S(2)}, u32[]{:S(2)}) %collective-permute-start.22) | collective-permute-done | bytes 98336 | tf_op jit(solution)/shard_map/ppermute | solution.py:399
  57.6 1.4 %collective-permute-start.27 = (bf16[4,32,128]{2,1,0:T(8,128)(2,1)S(1)}, bf16[4,32,128]{2,1,0:T(8,128)(2,1)S(1)}, u32[]{:S(2)}, u32[]{:S(2)}) collective-permute-start(bf16[4,32,128]{2,1,0:T(8,128)(2,1)S(1)} %get-tuple-element.110), channel_id=1, source_target_pairs={{0,4},{1,2},{2,1},{3,7},{4,0},{5,6},{6,5},{7,3},{8,12},{9,10},{10,... | collective-permute-start | bytes 98312 | tf_op jit(solution)/shard_map/ppermute | solution.py:399
  58.9 2.5 %collective-permute-done.26.near_ends = bf16[4,32,128]{2,1,0:T(8,128)(2,1)S(1)} collective-permute-done((bf16[4,32,128]{2,1,0:T(8,128)(2,1)S(1)}, bf16[4,32,128]{2,1,0:T(8,128)(2,1)S(1)}, u32[]{:S(2)}, u32[]{:S(2)}) %collective-permute-start.26) | collective-permute-done | bytes 32800 | tf_op jit(solution)/shard_map/ppermute | solution.py:399
  61.6 1.6 %one_step.7 = (f32[60,32,128]{2,1,0:T(8,128)S(1)}, f32[61,32,128]{2,1,0:T(8,128)S(1)}, bf16[6,32,128]{2,1,0:T(8,128)(2,1)S(1)}, bf16[6,32,128]{2,1,0:T(8,128)(2,1)S(1)}, f32[33,32,128]{2,1,0:T(8,128)S(1)}) custom-call(s32[7]{0:T(128)S(4)} %get-tuple-element.66.info_ref, s32[128]{0:T(128)S(4)} %get-tuple-element.67.rows_ref, ...), custom_call_target="tpu_custom_call" | custom-call | flops 268435456 | bytes 1048576 | tf_op jit(solution)/shard_map/one_step/pallas_call | solution.py:419
  63.3 1.1 %collective-permute-done.29.pair_in = bf16[6,32,128]{2,1,0:T(8,128)(2,1)S(1)} collective-permute-done((bf16[6,32,128]{2,1,0:T(8,128)(2,1)S(1)}, bf16[6,32,128]{2,1,0:T(8,128)(2,1)S(1)}, u32[]{:S(2)}, u32[]{:S(2)}) %collective-permute-start.29) | collective-permute-done | bytes 49184 | tf_op jit(solution)/shard_map/ppermute | solution.py:399
  64.6 1.3 %collective-permute-start.31 = (bf16[7,32,128]{2,1,0:T(8,128)(2,1)S(1)}, bf16[7,32,128]{2,1,0:T(8,128)(2,1)S(1)}, u32[]{:S(2)}, u32[]{:S(2)}) collective-permute-start(bf16[7,32,128]{2,1,0:T(8,128)(2,1)S(1)} %get-tuple-element.116), channel_id=1, source_target_pairs={{0,4},{1,2},{2,1},{3,7},{4,0},{5,6},{6,5},{7,3},{8,12},{9,10},{10,... | collective-permute-start | bytes 172040 | tf_op jit(solution)/shard_map/ppermute | solution.py:399
  65.9 0.8 %slice.35 = f32[32,32,128]{2,1,0:T(8,128)} slice(f32[33,32,128]{2,1,0:T(8,128)S(1)} %get-tuple-element.119), slice={[0:32], [0:32], [0:128]} | slice | bytes 1048576 | tf_op jit(solution)/shard_map/slice | solution.py:568
  66.7 2.2 %collective-permute-done.28.next_in = bf16[6,32,128]{2,1,0:T(8,128)(2,1)S(1)} collective-permute-done((bf16[6,32,128]{2,1,0:T(8,128)(2,1)S(1)}, bf16[6,32,128]{2,1,0:T(8,128)(2,1)S(1)}, u32[]{:S(2)}, u32[]{:S(2)}) %collective-permute-start.28) | collective-permute-done | bytes 49184 | tf_op jit(solution)/shard_map/ppermute | solution.py:399
  69.1 1.3 %collective-permute-start.33 = (bf16[1,32,128]{2,1,0:T(8,128)(2,1)S(1)}, bf16[1,32,128]{2,1,0:T(8,128)(2,1)S(1)}, u32[]{:S(2)}, u32[]{:S(2)}) collective-permute-start(bf16[1,32,128]{2,1,0:T(8,128)(2,1)S(1)} %get-tuple-element.118), channel_id=1, source_target_pairs={{0,4},{1,2},{2,1},{3,7},{4,0},{5,6},{6,5},{7,3},{8,12},{9,10},{10,... | collective-permute-start | bytes 24584 | tf_op jit(solution)/shard_map/ppermute | solution.py:399
  70.4 0.7 inner_rows.1.rest_4_
  71.1 1.6 %collective-permute-done.32.rest_2_ = bf16[1,32,128]{2,1,0:T(8,128)(2,1)S(1)} collective-permute-done((bf16[1,32,128]{2,1,0:T(8,128)(2,1)S(1)}, bf16[1,32,128]{2,1,0:T(8,128)(2,1)S(1)}, u32[]{:S(2)}, u32[]{:S(2)}) %collective-permute-start.32) | collective-permute-done | bytes 8224 | tf_op jit(solution)/shard_map/ppermute | solution.py:399
  72.8 0.8 %outer_rows.1 = f32[4,8,32,128]{3,2,1,0:T(8,128)} custom-call(s32[7]{0:T(128)S(4)} %get-tuple-element.66.info_ref, f32[60,32,128]{2,1,0:T(8,128)S(1)} %get-tuple-element.111.x_in, f32[61,32,128]{2,1,0:T(8,128)S(1)} %get-tuple-element.112.grad_in, bf16[6,32,128]{2,1,0:T(8,128)(2,1)S(1)} %collective-permute-done.28.next_in, ...), custom_call_target="tpu_custom_call", output_to_operand_aliasing={{}: (9, {})} | custom-call | flops 268435456 | bytes 1048576 | tf_op jit(solution)/shard_map/outer_rows/pallas_call | solution.py:537
  (52 shorter events, 1.8 us)
Async XLA Ops:
  1.7 5.5 %collective-permute-start = (bf16[8,32,128]{2,1,0:T(8,128)(2,1)S(1)}, bf16[8,32,128]{2,1,0:T(8,128)(2,1)S(1)}, u32[]{:S(2)}, u32[]{:S(2)}) collective-permute-start(bf16[8,32,128]{2,1,0:T(8,128)(2,1)S(1)} %get-tuple-element.63), channel_id=1, source_target_pairs={{0,1},{1,0},{2,3},{3,2},{4,5},{5,4},{6,7},{7,6},{8,9},{9,8},{10,11... | collective-permute-start | bytes 196616 | tf_op jit(solution)/shard_map/ppermute | solution.py:399
  2.3 4.9 %collective-permute-start.1 = (bf16[8,32,128]{2,1,0:T(8,128)(2,1)S(1)}, bf16[8,32,128]{2,1,0:T(8,128)(2,1)S(1)}, u32[]{:S(2)}, u32[]{:S(2)}) collective-permute-start(bf16[8,32,128]{2,1,0:T(8,128)(2,1)S(1)} %get-tuple-element.64), channel_id=1, source_target_pairs={{0,4},{1,2},{2,1},{3,7},{4,0},{5,6},{6,5},{7,3},{8,12},{9,10},{10,... | collective-permute-start | bytes 196616 | tf_op jit(solution)/shard_map/ppermute | solution.py:399
  7.3 5.7 %collective-permute-start.2 = (bf16[6,32,128]{2,1,0:T(8,128)(2,1)S(1)}, bf16[6,32,128]{2,1,0:T(8,128)(2,1)S(1)}, u32[]{:S(2)}, u32[]{:S(2)}) collective-permute-start(bf16[6,32,128]{2,1,0:T(8,128)(2,1)S(1)} %get-tuple-element.73), channel_id=1, source_target_pairs={{0,1},{1,0},{2,3},{3,2},{4,8},{5,9},{6,10},{7,11},{8,4},{9,5},{10,... | collective-permute-start | bytes 147464 | tf_op jit(solution)/shard_map/ppermute | solution.py:399
  10.5 2.5 %collective-permute-start.3 = (bf16[6,32,128]{2,1,0:T(8,128)(2,1)S(1)}, bf16[6,32,128]{2,1,0:T(8,128)(2,1)S(1)}, u32[]{:S(2)}, u32[]{:S(2)}) collective-permute-start(bf16[6,32,128]{2,1,0:T(8,128)(2,1)S(1)} %get-tuple-element.74), channel_id=1, source_target_pairs={{0,4},{1,5},{2,6},{3,7},{4,0},{5,1},{6,2},{7,3},{8,12},{9,13},{10,... | collective-permute-start | bytes 147464 | tf_op jit(solution)/shard_map/ppermute | solution.py:399
  10.5 2.5 %copy-start = (f32[4,8,32,128]{3,2,1,0:T(8,128)S(1)}, f32[4,8,32,128]{3,2,1,0:T(8,128)}, u32[]{:S(2)}) copy-start(f32[4,8,32,128]{3,2,1,0:T(8,128)} %param.7) | copy-start | bytes 1572868
  10.5 2.5 %copy-start.1 = (f32[4,8,32,128]{3,2,1,0:T(8,128)S(1)}, f32[4,8,32,128]{3,2,1,0:T(8,128)}, u32[]{:S(2)}) copy-start(f32[4,8,32,128]{3,2,1,0:T(8,128)} %param.6) | copy-start | bytes 1572868
  14.4 3.3 %collective-permute-start.5 = (bf16[12,32,128]{2,1,0:T(8,128)(2,1)S(1)}, bf16[12,32,128]{2,1,0:T(8,128)(2,1)S(1)}, u32[]{:S(2)}, u32[]{:S(2)}) collective-permute-start(bf16[12,32,128]{2,1,0:T(8,128)(2,1)S(1)} %get-tuple-element.82), channel_id=1, source_target_pairs={{0,4},{1,5},{2,6},{3,7},{4,0},{5,1},{6,2},{7,3},{8,12},{9,13},{10,... | collective-permute-start | bytes 294920 | tf_op jit(solution)/shard_map/ppermute | solution.py:399
  14.5 6.2 %collective-permute-start.4 = (bf16[12,32,128]{2,1,0:T(8,128)(2,1)S(1)}, bf16[12,32,128]{2,1,0:T(8,128)(2,1)S(1)}, u32[]{:S(2)}, u32[]{:S(2)}) collective-permute-start(bf16[12,32,128]{2,1,0:T(8,128)(2,1)S(1)} %get-tuple-element.81), channel_id=1, source_target_pairs={{0,1},{1,0},{2,3},{3,2},{4,8},{5,9},{6,10},{7,11},{8,4},{9,5},{10,... | collective-permute-start | bytes 294920 | tf_op jit(solution)/shard_map/ppermute | solution.py:399
  17.7 7.5 %collective-permute-start.6 = (bf16[16,32,128]{2,1,0:T(8,128)(2,1)S(1)}, bf16[16,32,128]{2,1,0:T(8,128)(2,1)S(1)}, u32[]{:S(2)}, u32[]{:S(2)}) collective-permute-start(bf16[16,32,128]{2,1,0:T(8,128)(2,1)S(1)} %get-tuple-element.83), channel_id=1, source_target_pairs={{0,1},{1,0},{2,3},{3,2},{4,5},{5,4},{6,7},{7,6},{8,9},{9,8},{10,11... | collective-permute-start | bytes 393224 | tf_op jit(solution)/shard_map/ppermute | solution.py:399
  18.3 6.9 %collective-permute-start.7 = (bf16[16,32,128]{2,1,0:T(8,128)(2,1)S(1)}, bf16[16,32,128]{2,1,0:T(8,128)(2,1)S(1)}, u32[]{:S(2)}, u32[]{:S(2)}) collective-permute-start(bf16[16,32,128]{2,1,0:T(8,128)(2,1)S(1)} %get-tuple-element.84), channel_id=1, source_target_pairs={{0,4},{1,2},{2,1},{3,7},{4,0},{5,6},{6,5},{7,3},{8,12},{9,10},{10,... | collective-permute-start | bytes 393224 | tf_op jit(solution)/shard_map/ppermute | solution.py:399
  20.7 4.0 %collective-permute-start.8 = (bf16[4,32,128]{2,1,0:T(8,128)(2,1)S(1)}, bf16[4,32,128]{2,1,0:T(8,128)(2,1)S(1)}, u32[]{:S(2)}, u32[]{:S(2)}) collective-permute-start(bf16[4,32,128]{2,1,0:T(8,128)(2,1)S(1)} %get-tuple-element.85), channel_id=1, source_target_pairs={{0,1},{1,0},{2,3},{3,2},{4,5},{5,4},{6,7},{7,6},{8,9},{9,8},{10,11... | collective-permute-start | bytes 98312 | tf_op jit(solution)/shard_map/ppermute | solution.py:399
  21.3 3.9 %collective-permute-start.9 = (bf16[4,32,128]{2,1,0:T(8,128)(2,1)S(1)}, bf16[4,32,128]{2,1,0:T(8,128)(2,1)S(1)}, u32[]{:S(2)}, u32[]{:S(2)}) collective-permute-start(bf16[4,32,128]{2,1,0:T(8,128)(2,1)S(1)} %get-tuple-element.86), channel_id=1, source_target_pairs={{0,4},{1,2},{2,1},{3,7},{4,0},{5,6},{6,5},{7,3},{8,12},{9,10},{10,... | collective-permute-start | bytes 98312 | tf_op jit(solution)/shard_map/ppermute | solution.py:399
  26.8 1.9 %collective-permute-start.11 = (bf16[12,32,128]{2,1,0:T(8,128)(2,1)S(1)}, bf16[12,32,128]{2,1,0:T(8,128)(2,1)S(1)}, u32[]{:S(2)}, u32[]{:S(2)}) collective-permute-start(bf16[12,32,128]{2,1,0:T(8,128)(2,1)S(1)} %get-tuple-element.90), channel_id=1, source_target_pairs={{0,4},{1,5},{2,6},{3,7},{4,0},{5,1},{6,2},{7,3},{8,12},{9,13},{10,... | collective-permute-start | bytes 294920 | tf_op jit(solution)/shard_map/ppermute | solution.py:399
  26.9 6.2 %collective-permute-start.10 = (bf16[12,32,128]{2,1,0:T(8,128)(2,1)S(1)}, bf16[12,32,128]{2,1,0:T(8,128)(2,1)S(1)}, u32[]{:S(2)}, u32[]{:S(2)}) collective-permute-start(bf16[12,32,128]{2,1,0:T(8,128)(2,1)S(1)} %get-tuple-element.89), channel_id=1, source_target_pairs={{0,1},{1,0},{2,3},{3,2},{4,8},{5,9},{6,10},{7,11},{8,4},{9,5},{10,... | collective-permute-start | bytes 294920 | tf_op jit(solution)/shard_map/ppermute | solution.py:399
  28.8 8.5 %collective-permute-start.12 = (bf16[16,32,128]{2,1,0:T(8,128)(2,1)S(1)}, bf16[16,32,128]{2,1,0:T(8,128)(2,1)S(1)}, u32[]{:S(2)}, u32[]{:S(2)}) collective-permute-start(bf16[16,32,128]{2,1,0:T(8,128)(2,1)S(1)} %get-tuple-element.91), channel_id=1, source_target_pairs={{0,1},{1,0},{2,3},{3,2},{4,5},{5,4},{6,7},{7,6},{8,9},{9,8},{10,11... | collective-permute-start | bytes 393224 | tf_op jit(solution)/shard_map/ppermute | solution.py:399
  29.1 8.2 %collective-permute-start.13 = (bf16[16,32,128]{2,1,0:T(8,128)(2,1)S(1)}, bf16[16,32,128]{2,1,0:T(8,128)(2,1)S(1)}, u32[]{:S(2)}, u32[]{:S(2)}) collective-permute-start(bf16[16,32,128]{2,1,0:T(8,128)(2,1)S(1)} %get-tuple-element.92), channel_id=1, source_target_pairs={{0,4},{1,2},{2,1},{3,7},{4,0},{5,6},{6,5},{7,3},{8,12},{9,10},{10,... | collective-permute-start | bytes 393224 | tf_op jit(solution)/shard_map/ppermute | solution.py:399
  33.2 4.0 %collective-permute-start.14 = (bf16[4,32,128]{2,1,0:T(8,128)(2,1)S(1)}, bf16[4,32,128]{2,1,0:T(8,128)(2,1)S(1)}, u32[]{:S(2)}, u32[]{:S(2)}) collective-permute-start(bf16[4,32,128]{2,1,0:T(8,128)(2,1)S(1)} %get-tuple-element.93), channel_id=1, source_target_pairs={{0,1},{1,0},{2,3},{3,2},{4,5},{5,4},{6,7},{7,6},{8,9},{9,8},{10,11... | collective-permute-start | bytes 98312 | tf_op jit(solution)/shard_map/ppermute | solution.py:399
  33.3 4.0 %collective-permute-start.15 = (bf16[4,32,128]{2,1,0:T(8,128)(2,1)S(1)}, bf16[4,32,128]{2,1,0:T(8,128)(2,1)S(1)}, u32[]{:S(2)}, u32[]{:S(2)}) collective-permute-start(bf16[4,32,128]{2,1,0:T(8,128)(2,1)S(1)} %get-tuple-element.94), channel_id=1, source_target_pairs={{0,4},{1,2},{2,1},{3,7},{4,0},{5,6},{6,5},{7,3},{8,12},{9,10},{10,... | collective-permute-start | bytes 98312 | tf_op jit(solution)/shard_map/ppermute | solution.py:399
  39.1 1.4 %collective-permute-start.17 = (bf16[12,32,128]{2,1,0:T(8,128)(2,1)S(1)}, bf16[12,32,128]{2,1,0:T(8,128)(2,1)S(1)}, u32[]{:S(2)}, u32[]{:S(2)}) collective-permute-start(bf16[12,32,128]{2,1,0:T(8,128)(2,1)S(1)} %get-tuple-element.98), channel_id=1, source_target_pairs={{0,4},{1,5},{2,6},{3,7},{4,0},{5,1},{6,2},{7,3},{8,12},{9,13},{10,... | collective-permute-start | bytes 294920 | tf_op jit(solution)/shard_map/ppermute | solution.py:399
  39.1 6.2 %collective-permute-start.16 = (bf16[12,32,128]{2,1,0:T(8,128)(2,1)S(1)}, bf16[12,32,128]{2,1,0:T(8,128)(2,1)S(1)}, u32[]{:S(2)}, u32[]{:S(2)}) collective-permute-start(bf16[12,32,128]{2,1,0:T(8,128)(2,1)S(1)} %get-tuple-element.97), channel_id=1, source_target_pairs={{0,1},{1,0},{2,3},{3,2},{4,8},{5,9},{6,10},{7,11},{8,4},{9,5},{10,... | collective-permute-start | bytes 294920 | tf_op jit(solution)/shard_map/ppermute | solution.py:399
  40.5 9.0 %collective-permute-start.18 = (bf16[16,32,128]{2,1,0:T(8,128)(2,1)S(1)}, bf16[16,32,128]{2,1,0:T(8,128)(2,1)S(1)}, u32[]{:S(2)}, u32[]{:S(2)}) collective-permute-start(bf16[16,32,128]{2,1,0:T(8,128)(2,1)S(1)} %get-tuple-element.99), channel_id=1, source_target_pairs={{0,1},{1,0},{2,3},{3,2},{4,5},{5,4},{6,7},{7,6},{8,9},{9,8},{10,11... | collective-permute-start | bytes 393224 | tf_op jit(solution)/shard_map/ppermute | solution.py:399
  40.6 8.9 %collective-permute-start.19 = (bf16[16,32,128]{2,1,0:T(8,128)(2,1)S(1)}, bf16[16,32,128]{2,1,0:T(8,128)(2,1)S(1)}, u32[]{:S(2)}, u32[]{:S(2)}) collective-permute-start(bf16[16,32,128]{2,1,0:T(8,128)(2,1)S(1)} %get-tuple-element.100), channel_id=1, source_target_pairs={{0,4},{1,2},{2,1},{3,7},{4,0},{5,6},{6,5},{7,3},{8,12},{9,10},{10,... | collective-permute-start | bytes 393224 | tf_op jit(solution)/shard_map/ppermute | solution.py:399
  45.4 4.0 %collective-permute-start.20 = (bf16[4,32,128]{2,1,0:T(8,128)(2,1)S(1)}, bf16[4,32,128]{2,1,0:T(8,128)(2,1)S(1)}, u32[]{:S(2)}, u32[]{:S(2)}) collective-permute-start(bf16[4,32,128]{2,1,0:T(8,128)(2,1)S(1)} %get-tuple-element.101), channel_id=1, source_target_pairs={{0,1},{1,0},{2,3},{3,2},{4,5},{5,4},{6,7},{7,6},{8,9},{9,8},{10,11... | collective-permute-start | bytes 98312 | tf_op jit(solution)/shard_map/ppermute | solution.py:399
  45.5 4.0 %collective-permute-start.21 = (bf16[4,32,128]{2,1,0:T(8,128)(2,1)S(1)}, bf16[4,32,128]{2,1,0:T(8,128)(2,1)S(1)}, u32[]{:S(2)}, u32[]{:S(2)}) collective-permute-start(bf16[4,32,128]{2,1,0:T(8,128)(2,1)S(1)} %get-tuple-element.102), channel_id=1, source_target_pairs={{0,4},{1,2},{2,1},{3,7},{4,0},{5,6},{6,5},{7,3},{8,12},{9,10},{10,... | collective-permute-start | bytes 98312 | tf_op jit(solution)/shard_map/ppermute | solution.py:399
  51.1 1.4 %collective-permute-start.23 = (bf16[12,32,128]{2,1,0:T(8,128)(2,1)S(1)}, bf16[12,32,128]{2,1,0:T(8,128)(2,1)S(1)}, u32[]{:S(2)}, u32[]{:S(2)}) collective-permute-start(bf16[12,32,128]{2,1,0:T(8,128)(2,1)S(1)} %get-tuple-element.106), channel_id=1, source_target_pairs={{0,4},{1,5},{2,6},{3,7},{4,0},{5,1},{6,2},{7,3},{8,12},{9,13},{10,... | collective-permute-start | bytes 294920 | tf_op jit(solution)/shard_map/ppermute | solution.py:399
  51.2 6.2 %collective-permute-start.22 = (bf16[12,32,128]{2,1,0:T(8,128)(2,1)S(1)}, bf16[12,32,128]{2,1,0:T(8,128)(2,1)S(1)}, u32[]{:S(2)}, u32[]{:S(2)}) collective-permute-start(bf16[12,32,128]{2,1,0:T(8,128)(2,1)S(1)} %get-tuple-element.105), channel_id=1, source_target_pairs={{0,1},{1,0},{2,3},{3,2},{4,8},{5,9},{6,10},{7,11},{8,4},{9,5},{10,... | collective-permute-start | bytes 294920 | tf_op jit(solution)/shard_map/ppermute | solution.py:399
  52.5 9.0 %collective-permute-start.24 = (bf16[16,32,128]{2,1,0:T(8,128)(2,1)S(1)}, bf16[16,32,128]{2,1,0:T(8,128)(2,1)S(1)}, u32[]{:S(2)}, u32[]{:S(2)}) collective-permute-start(bf16[16,32,128]{2,1,0:T(8,128)(2,1)S(1)} %get-tuple-element.107), channel_id=1, source_target_pairs={{0,1},{1,0},{2,3},{3,2},{4,5},{5,4},{6,7},{7,6},{8,9},{9,8},{10,11... | collective-permute-start | bytes 393224 | tf_op jit(solution)/shard_map/ppermute | solution.py:399
  52.6 8.9 %collective-permute-start.25 = (bf16[16,32,128]{2,1,0:T(8,128)(2,1)S(1)}, bf16[16,32,128]{2,1,0:T(8,128)(2,1)S(1)}, u32[]{:S(2)}, u32[]{:S(2)}) collective-permute-start(bf16[16,32,128]{2,1,0:T(8,128)(2,1)S(1)} %get-tuple-element.108), channel_id=1, source_target_pairs={{0,4},{1,2},{2,1},{3,7},{4,0},{5,6},{6,5},{7,3},{8,12},{9,10},{10,... | collective-permute-start | bytes 393224 | tf_op jit(solution)/shard_map/ppermute | solution.py:399
  57.5 4.0 %collective-permute-start.26 = (bf16[4,32,128]{2,1,0:T(8,128)(2,1)S(1)}, bf16[4,32,128]{2,1,0:T(8,128)(2,1)S(1)}, u32[]{:S(2)}, u32[]{:S(2)}) collective-permute-start(bf16[4,32,128]{2,1,0:T(8,128)(2,1)S(1)} %get-tuple-element.109), channel_id=1, source_target_pairs={{0,1},{1,0},{2,3},{3,2},{4,5},{5,4},{6,7},{7,6},{8,9},{9,8},{10,11... | collective-permute-start | bytes 98312 | tf_op jit(solution)/shard_map/ppermute | solution.py:399
  57.6 4.0 %collective-permute-start.27 = (bf16[4,32,128]{2,1,0:T(8,128)(2,1)S(1)}, bf16[4,32,128]{2,1,0:T(8,128)(2,1)S(1)}, u32[]{:S(2)}, u32[]{:S(2)}) collective-permute-start(bf16[4,32,128]{2,1,0:T(8,128)(2,1)S(1)} %get-tuple-element.110), channel_id=1, source_target_pairs={{0,4},{1,2},{2,1},{3,7},{4,0},{5,6},{6,5},{7,3},{8,12},{9,10},{10,... | collective-permute-start | bytes 98312 | tf_op jit(solution)/shard_map/ppermute | solution.py:399
  63.2 1.3 %collective-permute-start.29 = (bf16[6,32,128]{2,1,0:T(8,128)(2,1)S(1)}, bf16[6,32,128]{2,1,0:T(8,128)(2,1)S(1)}, u32[]{:S(2)}, u32[]{:S(2)}) collective-permute-start(bf16[6,32,128]{2,1,0:T(8,128)(2,1)S(1)} %get-tuple-element.114), channel_id=1, source_target_pairs={{0,4},{1,5},{2,6},{3,7},{4,0},{5,1},{6,2},{7,3},{8,12},{9,13},{10,... | collective-permute-start | bytes 147464 | tf_op jit(solution)/shard_map/ppermute | solution.py:399
  63.3 5.7 %collective-permute-start.28 = (bf16[6,32,128]{2,1,0:T(8,128)(2,1)S(1)}, bf16[6,32,128]{2,1,0:T(8,128)(2,1)S(1)}, u32[]{:S(2)}, u32[]{:S(2)}) collective-permute-start(bf16[6,32,128]{2,1,0:T(8,128)(2,1)S(1)} %get-tuple-element.113), channel_id=1, source_target_pairs={{0,1},{1,0},{2,3},{3,2},{4,8},{5,9},{6,10},{7,11},{8,4},{9,5},{10,... | collective-permute-start | bytes 147464 | tf_op jit(solution)/shard_map/ppermute | solution.py:399
  64.5 8.3 %collective-permute-start.30 = (bf16[7,32,128]{2,1,0:T(8,128)(2,1)S(1)}, bf16[7,32,128]{2,1,0:T(8,128)(2,1)S(1)}, u32[]{:S(2)}, u32[]{:S(2)}) collective-permute-start(bf16[7,32,128]{2,1,0:T(8,128)(2,1)S(1)} %get-tuple-element.115), channel_id=1, source_target_pairs={{0,1},{1,0},{2,3},{3,2},{4,5},{5,4},{6,7},{7,6},{8,9},{9,8},{10,11... | collective-permute-start | bytes 172040 | tf_op jit(solution)/shard_map/ppermute | solution.py:399
  64.6 8.2 %collective-permute-start.31 = (bf16[7,32,128]{2,1,0:T(8,128)(2,1)S(1)}, bf16[7,32,128]{2,1,0:T(8,128)(2,1)S(1)}, u32[]{:S(2)}, u32[]{:S(2)}) collective-permute-start(bf16[7,32,128]{2,1,0:T(8,128)(2,1)S(1)} %get-tuple-element.116), channel_id=1, source_target_pairs={{0,4},{1,2},{2,1},{3,7},{4,0},{5,6},{6,5},{7,3},{8,12},{9,10},{10,... | collective-permute-start | bytes 172040 | tf_op jit(solution)/shard_map/ppermute | solution.py:399
  69.0 3.7 %collective-permute-start.32 = (bf16[1,32,128]{2,1,0:T(8,128)(2,1)S(1)}, bf16[1,32,128]{2,1,0:T(8,128)(2,1)S(1)}, u32[]{:S(2)}, u32[]{:S(2)}) collective-permute-start(bf16[1,32,128]{2,1,0:T(8,128)(2,1)S(1)} %get-tuple-element.117), channel_id=1, source_target_pairs={{0,1},{1,0},{2,3},{3,2},{4,5},{5,4},{6,7},{7,6},{8,9},{9,8},{10,11... | collective-permute-start | bytes 24584 | tf_op jit(solution)/shard_map/ppermute | solution.py:399
  69.1 3.7 %collective-permute-start.33 = (bf16[1,32,128]{2,1,0:T(8,128)(2,1)S(1)}, bf16[1,32,128]{2,1,0:T(8,128)(2,1)S(1)}, u32[]{:S(2)}, u32[]{:S(2)}) collective-permute-start(bf16[1,32,128]{2,1,0:T(8,128)(2,1)S(1)} %get-tuple-element.118), channel_id=1, source_target_pairs={{0,4},{1,2},{2,1},{3,7},{4,0},{5,6},{6,5},{7,3},{8,12},{9,10},{10,... | collective-permute-start | bytes 24584 | tf_op jit(solution)/shard_map/ppermute | solution.py:399

commit v2 on v1

--- a/solution.py
+++ b/solution.py
@@ -183,16 +183,19 @@
                 turned_1[slot] = blocks_1[slot].T
 
 
-def first_kernel(sizes, info_ref, rows_ref, cols_ref, coef_ref, near_in, far_in, next_in, pair_in, observed_ref, blocks_0, blocks_1, turned_0, turned_1, x_ref, grad_ref, next_ref, pair_ref, low_ref, rlow_ref, residual_ref):
+def first_kernel(sizes, info_ref, rows_ref, cols_ref, coef_ref, near_in, far_in, next_in, pair_in, near_ends, far_ends, observed_ref, blocks_0, blocks_1, turned_0, turned_1, x_ref, grad_ref, next_ref, pair_ref, low_ref, rlow_ref, residual_ref):
     tile_x, tile_y, _ = sizes
     span = tile_y + 2
     even = info_ref[EVEN] == 1
     for row in range(tile_x + 2):
         for col in range(span):
-            if col == 0:
-                value = wide_value(jnp.where(even, next_in[row], pair_in[row]))
-            elif col == tile_y + 1:
-                value = wide_value(jnp.where(even, pair_in[row], next_in[row]))
+            if col in (0, tile_y + 1):
+                left = col == 0
+                if row in (0, tile_x + 1):
+                    value = came_along_narrow(info_ref, near_ends, far_ends, row == 0, 0 if left else 1)
+                else:
+                    from_next = even if left else jnp.logical_not(even)
+                    value = wide_value(jnp.where(from_next, next_in[row - 1], pair_in[row - 1]))
             elif row == 0:
                 value = came_along_narrow(info_ref, near_in, far_in, True, col - 1)
             elif row == tile_x + 1:
@@ -480,22 +483,24 @@
         cost_estimate=pl.CostEstimate(flops=work, bytes_accessed=4 << 20, transcendentals=0),
         name="turn_blocks",
     )(info, in_hbm(blocks.reshape(slots, width, width), pltpu.HBM))
-    near, far_row, info = lax.optimization_barrier((near, far_row, info))
-    above = jnp.where(row_even, far_row, near)
-    below = jnp.where(row_even, near, far_row)
     left, right = lax.optimization_barrier((coefficients[:, 0], coefficients[:, tile_y - 1]))
     left, right = cast_low(left), cast_low(right)
-    sides = []
-    for col, edge in ((0, left), (tile_y - 1, right)):
-        sides.append(jnp.concatenate([above[col : col + 1], edge, below[col : col + 1]], axis=0))
     next_out, pair_out = lax.optimization_barrier(
-        (jnp.where(even, sides[0], sides[1]), jnp.where(even, sides[1], sides[0]))
+        (jnp.where(even, left, right), jnp.where(even, right, left))
     )
     next_in, pair_in = along_wide(next_out, pair_out)
+    next_in, pair_in, info = lax.optimization_barrier((next_in, pair_in, info))
+    beside = (jnp.where(even, next_in, pair_in), jnp.where(even, pair_in, next_in))
+    upper = jnp.stack([side[0] for side in beside])
+    lower = jnp.stack([side[tile_x - 1] for side in beside])
+    near_out, far_out = lax.optimization_barrier(
+        (jnp.where(row_even, lower, upper), jnp.where(row_even, upper, lower))
+    )
+    ends = along_narrow(near_out, far_out)
     x, grad, next_out, pair_out = call(
         functools.partial(first_kernel, sizes),
         "first_step",
-        [info, row_ids, col_ids, coefficients.reshape(own, frames, width), near, far_row, next_in, pair_in, seen, *operator],
+        [info, row_ids, col_ids, coefficients.reshape(own, frames, width), near, far_row, next_in, pair_in, *ends, seen, *operator],
         3,
         step_outputs(False),
         [low_scratch, rlow_scratch, residual_scratch],

time: 73.8 us -> 75.8 us (1.027)
  waiting for transfers between devices: 27.7 us -> 42 us
  starting transfers between devices: 28.6 us -> 16.5 us
    ppermute x34 -> x36, waiting for transfers between devices: 27.7 us -> 42 us  [send(): return lax.ppermute(value, ('wide', 'narrow'), ring)]
    ppermute x34 -> x36, starting transfers between devices: 28.6 us -> 16.5 us  [send(): return lax.ppermute(value, ('wide', 'narrow'), ring)]
  transfers between devices with their start and end apart: 34 -> 36, of which waited for: 19 -> 22; matrix products, arithmetic and copies ran while one was open for 2% -> 3% of each run, Pallas kernels for 5% -> 5%
where the time goes in v2:
time: 75.8 us; the launch traced here: 75.7 us
  waiting for transfers between devices  42 us (55%)
  starting transfers between devices  16.5 us (22%)
  Pallas kernels  12.5 us (16%)
  local copies, waits for them, and re-layouts  2.82 us (4%)
  between operations  1.79 us (2%)
    ppermute x36, waiting for transfers between devices, send(): return lax.ppermute(value, ('wide', 'narrow'), ring)  42 us
    ppermute x36, starting transfers between devices, send(): return lax.ppermute(value, ('wide', 'narrow'), ring)  16.5 us
    pallas_call x15, Pallas kernels, call(): pl.pallas_call(kernel, out_shape=outputs, in_specs=[smem] * scalars + [vm...  8 us
    pallas_call x1, Pallas kernels, local(): pl.pallas_call(turn_kernel, out_shape=[half_shape] * 4, in_specs=[smem, p...  1.96 us
  transfers between devices with their start and end apart: 36, of which 22 were waited for; matrix products, arithmetic and copies ran while one was open for 3% of the time, Pallas kernels for 5%

profile of v2, /device:TPU:26, one launch (start us, length us, event | category | flops | bytes accessed | tf_op | source)
XLA Modules:
  0.0 75.7 jit_solution(10974474145983442209)
XLA Ops:
  0.6 0.9 %slice_bitcast_fusion.2 = (bf16[4,32,128]{2,1,0:T(8,128)(2,1)S(1)}, bf16[4,32,128]{2,1,0:T(8,128)(2,1)S(1)}) fusion(f32[4,8,32,128]{3,2,1,0:T(8,128)} %param.6), kind=kLoop, calls=%fused_computation.4 | loop fusion | bytes 131072 | tf_op jit(solution)/shard_map/squeeze | solution.py:486
  1.6 3.7 %collective-permute-start = (bf16[4,32,128]{2,1,0:T(8,128)(2,1)S(1)}, bf16[4,32,128]{2,1,0:T(8,128)(2,1)S(1)}, u32[]{:S(2)}, u32[]{:S(2)}) collective-permute-start(bf16[4,32,128]{2,1,0:T(8,128)(2,1)S(1)} %get-tuple-element.65), channel_id=1, source_target_pairs={{0,1},{1,0},{2,3},{3,2},{4,8},{5,9},{6,10},{7,11},{8,4},{9,5},{10,... | collective-permute-start | bytes 98312 | tf_op jit(solution)/shard_map/ppermute | solution.py:402
  5.3 1.0 %slice_bitcast_fusion = (bf16[8,32,128]{2,1,0:T(8,128)(2,1)S(1)}, bf16[8,32,128]{2,1,0:T(8,128)(2,1)S(1)}) fusion(f32[4,8,32,128]{3,2,1,0:T(8,128)} %param.6), kind=kLoop, calls=%fused_computation.2 | loop fusion | bytes 262144 | tf_op jit(solution)/shard_map/squeeze | solution.py:450
  6.3 0.6 collective-permute-start.2
  6.9 2.2 %collective-permute-start.3 = (bf16[8,32,128]{2,1,0:T(8,128)(2,1)S(1)}, bf16[8,32,128]{2,1,0:T(8,128)(2,1)S(1)}, u32[]{:S(2)}, u32[]{:S(2)}) collective-permute-start(bf16[8,32,128]{2,1,0:T(8,128)(2,1)S(1)} %get-tuple-element.74), channel_id=1, source_target_pairs={{0,4},{1,2},{2,1},{3,7},{4,0},{5,6},{6,5},{7,3},{8,12},{9,10},{10,... | collective-permute-start | bytes 196616 | tf_op jit(solution)/shard_map/ppermute | solution.py:402
  9.9 1.1 %plan_slots.1 = (s32[7]{0:T(128)S(4)}, s32[128]{0:T(128)S(4)}, s32[128]{0:T(128)S(4)}) custom-call(s32[6]{0:T(128)S(1)} %convert_element_type.17.flags_ref, s32[1,1]{1,0:T(1,128)S(6)} %copy.14.live_ref, s32[128]{0:T(128)} %bitcast.32, s32[128]{0:T(128)} %bitcast.33), custom_call_target="tpu_custom_call" | custom-call | flops 268435456 | bytes 1048576 | tf_op jit(solution)/shard_map/plan_slots/pallas_call | solution.py:456
  11.1 1.0 %collective-permute-start.5 = (bf16[2,32,128]{2,1,0:T(8,128)(2,1)S(1)}, bf16[2,32,128]{2,1,0:T(8,128)(2,1)S(1)}, u32[]{:S(2)}, u32[]{:S(2)}) collective-permute-start(bf16[2,32,128]{2,1,0:T(8,128)(2,1)S(1)} %get-tuple-element.78), channel_id=1, source_target_pairs={{0,4},{1,2},{2,1},{3,7},{4,0},{5,6},{6,5},{7,3},{8,12},{9,10},{10,... | collective-permute-start | bytes 49160 | tf_op jit(solution)/shard_map/ppermute | solution.py:402
  12.2 2.0 %turn_blocks.1 = (bf16[64,128,128]{2,1,0:T(8,128)(2,1)S(1)}, bf16[64,128,128]{2,1,0:T(8,128)(2,1)S(1)}, bf16[64,128,128]{2,1,0:T(8,128)(2,1)S(1)}, bf16[64,128,128]{2,1,0:T(8,128)(2,1)S(1)}) custom-call(s32[7]{0:T(128)S(4)} %get-tuple-element.68.info_ref, bf16[128,128,128]{2,1,0:T(8,128)(2,1)} %bitcast.30), custom_call_target="tpu_custom_call" | custom-call | flops 268435456 | bytes 4194304 | tf_op jit(solution)/shard_map/turn_blocks/pallas_call | solution.py:476
  14.1 0.7 collective-permute-done.4.near_ends
  15.0 1.4 %first_step.1 = (f32[60,32,128]{2,1,0:T(8,128)S(1)}, f32[61,32,128]{2,1,0:T(8,128)S(1)}, bf16[12,32,128]{2,1,0:T(8,128)(2,1)S(1)}, bf16[12,32,128]{2,1,0:T(8,128)(2,1)S(1)}) custom-call(s32[7]{0:T(128)S(4)} %get-tuple-element.68.info_ref, s32[128]{0:T(128)S(4)} %get-tuple-element.69.rows_ref, s32[128]{0:T(128)S(4)} %get-tuple-element.70.cols_ref, ...), custom_call_target="tpu_custom_call" | custom-call | flops 268435456 | bytes 1048576 | tf_op jit(solution)/shard_map/first_step/pallas_call | solution.py:422
  16.4 0.8 %collective-permute-start.6 = (bf16[12,32,128]{2,1,0:T(8,128)(2,1)S(1)}, bf16[12,32,128]{2,1,0:T(8,128)(2,1)S(1)}, u32[]{:S(2)}, u32[]{:S(2)}) collective-permute-start(bf16[12,32,128]{2,1,0:T(8,128)(2,1)S(1)} %get-tuple-element.85), channel_id=1, source_target_pairs={{0,1},{1,0},{2,3},{3,2},{4,8},{5,9},{6,10},{7,11},{8,4},{9,5},{10,... | collective-permute-start | bytes 294920 | tf_op jit(solution)/shard_map/ppermute | solution.py:402
  17.2 0.5 collective-permute-done.7.pair_in
  17.8 0.4 collective-permute-start.8
  18.2 0.7 collective-permute-start.9
  18.9 3.8 %collective-permute-done.6.next_in = bf16[12,32,128]{2,1,0:T(8,128)(2,1)S(1)} collective-permute-done((bf16[12,32,128]{2,1,0:T(8,128)(2,1)S(1)}, bf16[12,32,128]{2,1,0:T(8,128)(2,1)S(1)}, u32[]{:S(2)}, u32[]{:S(2)}) %collective-permute-start.6) | collective-permute-done | bytes 98336 | tf_op jit(solution)/shard_map/ppermute | solution.py:402
  22.7 0.7 collective-permute-start.10
  23.4 0.5 collective-permute-start.11
  23.8 2.9 %collective-permute-done.10.near_ends = bf16[4,32,128]{2,1,0:T(8,128)(2,1)S(1)} collective-permute-done((bf16[4,32,128]{2,1,0:T(8,128)(2,1)S(1)}, bf16[4,32,128]{2,1,0:T(8,128)(2,1)S(1)}, u32[]{:S(2)}, u32[]{:S(2)}) %collective-permute-start.10) | collective-permute-done | bytes 32800 | tf_op jit(solution)/shard_map/ppermute | solution.py:402
  26.7 0.6 collective-permute-done.11.far_ends
  27.3 1.6 %one_step.4 = (f32[60,32,128]{2,1,0:T(8,128)S(1)}, f32[61,32,128]{2,1,0:T(8,128)S(1)}, bf16[12,32,128]{2,1,0:T(8,128)(2,1)S(1)}, bf16[12,32,128]{2,1,0:T(8,128)(2,1)S(1)}) custom-call(s32[7]{0:T(128)S(4)} %get-tuple-element.68.info_ref, s32[128]{0:T(128)S(4)} %get-tuple-element.69.rows_ref, s32[128]{0:T(128)S(4)} %get-tuple-element.70.cols_ref, ...), custom_call_target="tpu_custom_call" | custom-call | flops 268435456 | bytes 1048576 | tf_op jit(solution)/shard_map/one_step/pallas_call | solution.py:422
  29.1 1.2 %collective-permute-done.13.pair_in = bf16[12,32,128]{2,1,0:T(8,128)(2,1)S(1)} collective-permute-done((bf16[12,32,128]{2,1,0:T(8,128)(2,1)S(1)}, bf16[12,32,128]{2,1,0:T(8,128)(2,1)S(1)}, u32[]{:S(2)}, u32[]{:S(2)}) %collective-permute-start.13) | collective-permute-done | bytes 98336 | tf_op jit(solution)/shard_map/ppermute | solution.py:402
  30.3 0.1 collective-permute-start.14
  30.4 0.5 collective-permute-start.15
  30.9 4.3 %collective-permute-done.12.next_in = bf16[12,32,128]{2,1,0:T(8,128)(2,1)S(1)} collective-permute-done((bf16[12,32,128]{2,1,0:T(8,128)(2,1)S(1)}, bf16[12,32,128]{2,1,0:T(8,128)(2,1)S(1)}, u32[]{:S(2)}, u32[]{:S(2)}) %collective-permute-start.12) | collective-permute-done | bytes 98336 | tf_op jit(solution)/shard_map/ppermute | solution.py:402
  35.3 0.7 collective-permute-start.17
  36.0 3.2 %collective-permute-done.16.near_ends = bf16[4,32,128]{2,1,0:T(8,128)(2,1)S(1)} collective-permute-done((bf16[4,32,128]{2,1,0:T(8,128)(2,1)S(1)}, bf16[4,32,128]{2,1,0:T(8,128)(2,1)S(1)}, u32[]{:S(2)}, u32[]{:S(2)}) %collective-permute-start.16) | collective-permute-done | bytes 32800 | tf_op jit(solution)/shard_map/ppermute | solution.py:402
  39.2 0.3 collective-permute-done.17.far_ends
  39.5 1.6 %one_step.5 = (f32[60,32,128]{2,1,0:T(8,128)S(1)}, f32[61,32,128]{2,1,0:T(8,128)S(1)}, bf16[12,32,128]{2,1,0:T(8,128)(2,1)S(1)}, bf16[12,32,128]{2,1,0:T(8,128)(2,1)S(1)}) custom-call(s32[7]{0:T(128)S(4)} %get-tuple-element.68.info_ref, s32[128]{0:T(128)S(4)} %get-tuple-element.69.rows_ref, s32[128]{0:T(128)S(4)} %get-tuple-element.70.cols_ref, ...), custom_call_target="tpu_custom_call" | custom-call | flops 268435456 | bytes 1048576 | tf_op jit(solution)/shard_map/one_step/pallas_call | solution.py:422
  41.3 1.2 %collective-permute-done.19.pair_in = bf16[12,32,128]{2,1,0:T(8,128)(2,1)S(1)} collective-permute-done((bf16[12,32,128]{2,1,0:T(8,128)(2,1)S(1)}, bf16[12,32,128]{2,1,0:T(8,128)(2,1)S(1)}, u32[]{:S(2)}, u32[]{:S(2)}) %collective-permute-start.19) | collective-permute-done | bytes 98336 | tf_op jit(solution)/shard_map/ppermute | solution.py:402
  42.6 0.5 collective-permute-start.21
  43.1 4.3 %collective-permute-done.18.next_in = bf16[12,32,128]{2,1,0:T(8,128)(2,1)S(1)} collective-permute-done((bf16[12,32,128]{2,1,0:T(8,128)(2,1)S(1)}, bf16[12,32,128]{2,1,0:T(8,128)(2,1)S(1)}, u32[]{:S(2)}, u32[]{:S(2)}) %collective-permute-start.18) | collective-permute-done | bytes 98336 | tf_op jit(solution)/shard_map/ppermute | solution.py:402
  47.5 0.5 collective-permute-start.23
  48.1 3.4 %collective-permute-done.22.near_ends = bf16[4,32,128]{2,1,0:T(8,128)(2,1)S(1)} collective-permute-done((bf16[4,32,128]{2,1,0:T(8,128)(2,1)S(1)}, bf16[4,32,128]{2,1,0:T(8,128)(2,1)S(1)}, u32[]{:S(2)}, u32[]{:S(2)}) %collective-permute-start.22) | collective-permute-done | bytes 32800 | tf_op jit(solution)/shard_map/ppermute | solution.py:402
  51.5 1.6 %one_step.6 = (f32[60,32,128]{2,1,0:T(8,128)S(1)}, f32[61,32,128]{2,1,0:T(8,128)S(1)}, bf16[12,32,128]{2,1,0:T(8,128)(2,1)S(1)}, bf16[12,32,128]{2,1,0:T(8,128)(2,1)S(1)}) custom-call(s32[7]{0:T(128)S(4)} %get-tuple-element.68.info_ref, s32[128]{0:T(128)S(4)} %get-tuple-element.69.rows_ref, s32[128]{0:T(128)S(4)} %get-tuple-element.70.cols_ref, ...), custom_call_target="tpu_custom_call" | custom-call | flops 268435456 | bytes 1048576 | tf_op jit(solution)/shard_map/one_step/pallas_call | solution.py:422
  53.3 1.2 %collective-permute-done.25.pair_in = bf16[12,32,128]{2,1,0:T(8,128)(2,1)S(1)} collective-permute-done((bf16[12,32,128]{2,1,0:T(8,128)(2,1)S(1)}, bf16[12,32,128]{2,1,0:T(8,128)(2,1)S(1)}, u32[]{:S(2)}, u32[]{:S(2)}) %collective-permute-start.25) | collective-permute-done | bytes 98336 | tf_op jit(solution)/shard_map/ppermute | solution.py:402
  54.7 0.5 collective-permute-start.27
  55.2 4.3 %collective-permute-done.24.next_in = bf16[12,32,128]{2,1,0:T(8,128)(2,1)S(1)} collective-permute-done((bf16[12,32,128]{2,1,0:T(8,128)(2,1)S(1)}, bf16[12,32,128]{2,1,0:T(8,128)(2,1)S(1)}, u32[]{:S(2)}, u32[]{:S(2)}) %collective-permute-start.24) | collective-permute-done | bytes 98336 | tf_op jit(solution)/shard_map/ppermute | solution.py:402
  59.6 0.5 collective-permute-start.29
  60.1 3.4 %collective-permute-done.28.near_ends = bf16[4,32,128]{2,1,0:T(8,128)(2,1)S(1)} collective-permute-done((bf16[4,32,128]{2,1,0:T(8,128)(2,1)S(1)}, bf16[4,32,128]{2,1,0:T(8,128)(2,1)S(1)}, u32[]{:S(2)}, u32[]{:S(2)}) %collective-permute-start.28) | collective-permute-done | bytes 32800 | tf_op jit(solution)/shard_map/ppermute | solution.py:402
  63.6 1.6 %one_step.7 = (f32[60,32,128]{2,1,0:T(8,128)S(1)}, f32[61,32,128]{2,1,0:T(8,128)S(1)}, bf16[6,32,128]{2,1,0:T(8,128)(2,1)S(1)}, bf16[6,32,128]{2,1,0:T(8,128)(2,1)S(1)}, f32[33,32,128]{2,1,0:T(8,128)S(1)}) custom-call(s32[7]{0:T(128)S(4)} %get-tuple-element.68.info_ref, s32[128]{0:T(128)S(4)} %get-tuple-element.69.rows_ref, ...), custom_call_target="tpu_custom_call" | custom-call | flops 268435456 | bytes 1048576 | tf_op jit(solution)/shard_map/one_step/pallas_call | solution.py:422
  65.3 1.1 %collective-permute-done.31.pair_in = bf16[6,32,128]{2,1,0:T(8,128)(2,1)S(1)} collective-permute-done((bf16[6,32,128]{2,1,0:T(8,128)(2,1)S(1)}, bf16[6,32,128]{2,1,0:T(8,128)(2,1)S(1)}, u32[]{:S(2)}, u32[]{:S(2)}) %collective-permute-start.31) | collective-permute-done | bytes 49184 | tf_op jit(solution)/shard_map/ppermute | solution.py:402
  66.6 0.5 collective-permute-start.33
  67.1 0.8 %slice.35 = f32[32,32,128]{2,1,0:T(8,128)} slice(f32[33,32,128]{2,1,0:T(8,128)S(1)} %get-tuple-element.123), slice={[0:32], [0:32], [0:128]} | slice | bytes 1048576 | tf_op jit(solution)/shard_map/slice | solution.py:573
  67.9 3.0 %collective-permute-done.30.next_in = bf16[6,32,128]{2,1,0:T(8,128)(2,1)S(1)} collective-permute-done((bf16[6,32,128]{2,1,0:T(8,128)(2,1)S(1)}, bf16[6,32,128]{2,1,0:T(8,128)(2,1)S(1)}, u32[]{:S(2)}, u32[]{:S(2)}) %collective-permute-start.30) | collective-permute-done | bytes 49184 | tf_op jit(solution)/shard_map/ppermute | solution.py:402
  71.1 0.5 collective-permute-start.35
  71.6 0.7 inner_rows.1.rest_4_
  72.3 2.4 %collective-permute-done.34.rest_2_ = bf16[1,32,128]{2,1,0:T(8,128)(2,1)S(1)} collective-permute-done((bf16[1,32,128]{2,1,0:T(8,128)(2,1)S(1)}, bf16[1,32,128]{2,1,0:T(8,128)(2,1)S(1)}, u32[]{:S(2)}, u32[]{:S(2)}) %collective-permute-start.34) | collective-permute-done | bytes 8224 | tf_op jit(solution)/shard_map/ppermute | solution.py:402
  74.8 0.8 %outer_rows.1 = f32[4,8,32,128]{3,2,1,0:T(8,128)} custom-call(s32[7]{0:T(128)S(4)} %get-tuple-element.68.info_ref, f32[60,32,128]{2,1,0:T(8,128)S(1)} %get-tuple-element.115.x_in, f32[61,32,128]{2,1,0:T(8,128)S(1)} %get-tuple-element.116.grad_in, bf16[6,32,128]{2,1,0:T(8,128)(2,1)S(1)} %collective-permute-done.30.next_in, ...), custom_call_target="tpu_custom_call", output_to_operand_aliasing={{}: (9, {})} | custom-call | flops 268435456 | bytes 1048576 | tf_op jit(solution)/shard_map/outer_rows/pallas_call | solution.py:542
  (57 shorter events, 2.3 us)
Async XLA Ops:
  1.6 9.4 %collective-permute-start = (bf16[4,32,128]{2,1,0:T(8,128)(2,1)S(1)}, bf16[4,32,128]{2,1,0:T(8,128)(2,1)S(1)}, u32[]{:S(2)}, u32[]{:S(2)}) collective-permute-start(bf16[4,32,128]{2,1,0:T(8,128)(2,1)S(1)} %get-tuple-element.65), channel_id=1, source_target_pairs={{0,1},{1,0},{2,3},{3,2},{4,8},{5,9},{6,10},{7,11},{8,4},{9,5},{10,... | collective-permute-start | bytes 98312 | tf_op jit(solution)/shard_map/ppermute | solution.py:402
  5.3 5.7 %collective-permute-start.1 = (bf16[4,32,128]{2,1,0:T(8,128)(2,1)S(1)}, bf16[4,32,128]{2,1,0:T(8,128)(2,1)S(1)}, u32[]{:S(2)}, u32[]{:S(2)}) collective-permute-start(bf16[4,32,128]{2,1,0:T(8,128)(2,1)S(1)} %get-tuple-element.66), channel_id=1, source_target_pairs={{0,4},{1,5},{2,6},{3,7},{4,0},{5,1},{6,2},{7,3},{8,12},{9,13},{10,... | collective-permute-start | bytes 98312 | tf_op jit(solution)/shard_map/ppermute | solution.py:402
  6.3 8.6 %collective-permute-start.2 = (bf16[8,32,128]{2,1,0:T(8,128)(2,1)S(1)}, bf16[8,32,128]{2,1,0:T(8,128)(2,1)S(1)}, u32[]{:S(2)}, u32[]{:S(2)}) collective-permute-start(bf16[8,32,128]{2,1,0:T(8,128)(2,1)S(1)} %get-tuple-element.73), channel_id=1, source_target_pairs={{0,1},{1,0},{2,3},{3,2},{4,5},{5,4},{6,7},{7,6},{8,9},{9,8},{10,11... | collective-permute-start | bytes 196616 | tf_op jit(solution)/shard_map/ppermute | solution.py:402
  6.9 8.0 %collective-permute-start.3 = (bf16[8,32,128]{2,1,0:T(8,128)(2,1)S(1)}, bf16[8,32,128]{2,1,0:T(8,128)(2,1)S(1)}, u32[]{:S(2)}, u32[]{:S(2)}) collective-permute-start(bf16[8,32,128]{2,1,0:T(8,128)(2,1)S(1)} %get-tuple-element.74), channel_id=1, source_target_pairs={{0,4},{1,2},{2,1},{3,7},{4,0},{5,6},{6,5},{7,3},{8,12},{9,10},{10,... | collective-permute-start | bytes 196616 | tf_op jit(solution)/shard_map/ppermute | solution.py:402
  11.0 3.8 %collective-permute-start.4 = (bf16[2,32,128]{2,1,0:T(8,128)(2,1)S(1)}, bf16[2,32,128]{2,1,0:T(8,128)(2,1)S(1)}, u32[]{:S(2)}, u32[]{:S(2)}) collective-permute-start(bf16[2,32,128]{2,1,0:T(8,128)(2,1)S(1)} %get-tuple-element.77), channel_id=1, source_target_pairs={{0,1},{1,0},{2,3},{3,2},{4,5},{5,4},{6,7},{7,6},{8,9},{9,8},{10,11... | collective-permute-start | bytes 49160 | tf_op jit(solution)/shard_map/ppermute | solution.py:402
  11.1 3.8 %collective-permute-start.5 = (bf16[2,32,128]{2,1,0:T(8,128)(2,1)S(1)}, bf16[2,32,128]{2,1,0:T(8,128)(2,1)S(1)}, u32[]{:S(2)}, u32[]{:S(2)}) collective-permute-start(bf16[2,32,128]{2,1,0:T(8,128)(2,1)S(1)} %get-tuple-element.78), channel_id=1, source_target_pairs={{0,4},{1,2},{2,1},{3,7},{4,0},{5,6},{6,5},{7,3},{8,12},{9,10},{10,... | collective-permute-start | bytes 49160 | tf_op jit(solution)/shard_map/ppermute | solution.py:402
  12.2 2.8 %copy-start = (f32[4,8,32,128]{3,2,1,0:T(8,128)S(1)}, f32[4,8,32,128]{3,2,1,0:T(8,128)}, u32[]{:S(2)}) copy-start(f32[4,8,32,128]{3,2,1,0:T(8,128)} %param.7) | copy-start | bytes 1572868
  12.2 2.8 %copy-start.1 = (f32[4,8,32,128]{3,2,1,0:T(8,128)S(1)}, f32[4,8,32,128]{3,2,1,0:T(8,128)}, u32[]{:S(2)}) copy-start(f32[4,8,32,128]{3,2,1,0:T(8,128)} %param.6) | copy-start | bytes 1572868
  16.3 1.4 %collective-permute-start.7 = (bf16[12,32,128]{2,1,0:T(8,128)(2,1)S(1)}, bf16[12,32,128]{2,1,0:T(8,128)(2,1)S(1)}, u32[]{:S(2)}, u32[]{:S(2)}) collective-permute-start(bf16[12,32,128]{2,1,0:T(8,128)(2,1)S(1)} %get-tuple-element.86), channel_id=1, source_target_pairs={{0,4},{1,5},{2,6},{3,7},{4,0},{5,1},{6,2},{7,3},{8,12},{9,13},{10,... | collective-permute-start | bytes 294920 | tf_op jit(solution)/shard_map/ppermute | solution.py:402
  16.4 6.2 %collective-permute-start.6 = (bf16[12,32,128]{2,1,0:T(8,128)(2,1)S(1)}, bf16[12,32,128]{2,1,0:T(8,128)(2,1)S(1)}, u32[]{:S(2)}, u32[]{:S(2)}) collective-permute-start(bf16[12,32,128]{2,1,0:T(8,128)(2,1)S(1)} %get-tuple-element.85), channel_id=1, source_target_pairs={{0,1},{1,0},{2,3},{3,2},{4,8},{5,9},{6,10},{7,11},{8,4},{9,5},{10,... | collective-permute-start | bytes 294920 | tf_op jit(solution)/shard_map/ppermute | solution.py:402
  17.8 9.5 %collective-permute-start.8 = (bf16[16,32,128]{2,1,0:T(8,128)(2,1)S(1)}, bf16[16,32,128]{2,1,0:T(8,128)(2,1)S(1)}, u32[]{:S(2)}, u32[]{:S(2)}) collective-permute-start(bf16[16,32,128]{2,1,0:T(8,128)(2,1)S(1)} %get-tuple-element.87), channel_id=1, source_target_pairs={{0,1},{1,0},{2,3},{3,2},{4,5},{5,4},{6,7},{7,6},{8,9},{9,8},{10,11... | collective-permute-start | bytes 393224 | tf_op jit(solution)/shard_map/ppermute | solution.py:402
  18.2 9.1 %collective-permute-start.9 = (bf16[16,32,128]{2,1,0:T(8,128)(2,1)S(1)}, bf16[16,32,128]{2,1,0:T(8,128)(2,1)S(1)}, u32[]{:S(2)}, u32[]{:S(2)}) collective-permute-start(bf16[16,32,128]{2,1,0:T(8,128)(2,1)S(1)} %get-tuple-element.88), channel_id=1, source_target_pairs={{0,4},{1,2},{2,1},{3,7},{4,0},{5,6},{6,5},{7,3},{8,12},{9,10},{10,... | collective-permute-start | bytes 393224 | tf_op jit(solution)/shard_map/ppermute | solution.py:402
  22.7 4.0 %collective-permute-start.10 = (bf16[4,32,128]{2,1,0:T(8,128)(2,1)S(1)}, bf16[4,32,128]{2,1,0:T(8,128)(2,1)S(1)}, u32[]{:S(2)}, u32[]{:S(2)}) collective-permute-start(bf16[4,32,128]{2,1,0:T(8,128)(2,1)S(1)} %get-tuple-element.89), channel_id=1, source_target_pairs={{0,1},{1,0},{2,3},{3,2},{4,5},{5,4},{6,7},{7,6},{8,9},{9,8},{10,11... | collective-permute-start | bytes 98312 | tf_op jit(solution)/shard_map/ppermute | solution.py:402
  23.4 3.9 %collective-permute-start.11 = (bf16[4,32,128]{2,1,0:T(8,128)(2,1)S(1)}, bf16[4,32,128]{2,1,0:T(8,128)(2,1)S(1)}, u32[]{:S(2)}, u32[]{:S(2)}) collective-permute-start(bf16[4,32,128]{2,1,0:T(8,128)(2,1)S(1)} %get-tuple-element.90), channel_id=1, source_target_pairs={{0,4},{1,2},{2,1},{3,7},{4,0},{5,6},{6,5},{7,3},{8,12},{9,10},{10,... | collective-permute-start | bytes 98312 | tf_op jit(solution)/shard_map/ppermute | solution.py:402
  28.9 1.4 %collective-permute-start.13 = (bf16[12,32,128]{2,1,0:T(8,128)(2,1)S(1)}, bf16[12,32,128]{2,1,0:T(8,128)(2,1)S(1)}, u32[]{:S(2)}, u32[]{:S(2)}) collective-permute-start(bf16[12,32,128]{2,1,0:T(8,128)(2,1)S(1)} %get-tuple-element.94), channel_id=1, source_target_pairs={{0,4},{1,5},{2,6},{3,7},{4,0},{5,1},{6,2},{7,3},{8,12},{9,13},{10,... | collective-permute-start | bytes 294920 | tf_op jit(solution)/shard_map/ppermute | solution.py:402
  29.0 6.2 %collective-permute-start.12 = (bf16[12,32,128]{2,1,0:T(8,128)(2,1)S(1)}, bf16[12,32,128]{2,1,0:T(8,128)(2,1)S(1)}, u32[]{:S(2)}, u32[]{:S(2)}) collective-permute-start(bf16[12,32,128]{2,1,0:T(8,128)(2,1)S(1)} %get-tuple-element.93), channel_id=1, source_target_pairs={{0,1},{1,0},{2,3},{3,2},{4,8},{5,9},{6,10},{7,11},{8,4},{9,5},{10,... | collective-permute-start | bytes 294920 | tf_op jit(solution)/shard_map/ppermute | solution.py:402
  30.3 9.2 %collective-permute-start.14 = (bf16[16,32,128]{2,1,0:T(8,128)(2,1)S(1)}, bf16[16,32,128]{2,1,0:T(8,128)(2,1)S(1)}, u32[]{:S(2)}, u32[]{:S(2)}) collective-permute-start(bf16[16,32,128]{2,1,0:T(8,128)(2,1)S(1)} %get-tuple-element.95), channel_id=1, source_target_pairs={{0,1},{1,0},{2,3},{3,2},{4,5},{5,4},{6,7},{7,6},{8,9},{9,8},{10,11... | collective-permute-start | bytes 393224 | tf_op jit(solution)/shard_map/ppermute | solution.py:402
  30.4 9.1 %collective-permute-start.15 = (bf16[16,32,128]{2,1,0:T(8,128)(2,1)S(1)}, bf16[16,32,128]{2,1,0:T(8,128)(2,1)S(1)}, u32[]{:S(2)}, u32[]{:S(2)}) collective-permute-start(bf16[16,32,128]{2,1,0:T(8,128)(2,1)S(1)} %get-tuple-element.96), channel_id=1, source_target_pairs={{0,4},{1,2},{2,1},{3,7},{4,0},{5,6},{6,5},{7,3},{8,12},{9,10},{10,... | collective-permute-start | bytes 393224 | tf_op jit(solution)/shard_map/ppermute | solution.py:402
  35.2 4.0 %collective-permute-start.16 = (bf16[4,32,128]{2,1,0:T(8,128)(2,1)S(1)}, bf16[4,32,128]{2,1,0:T(8,128)(2,1)S(1)}, u32[]{:S(2)}, u32[]{:S(2)}) collective-permute-start(bf16[4,32,128]{2,1,0:T(8,128)(2,1)S(1)} %get-tuple-element.97), channel_id=1, source_target_pairs={{0,1},{1,0},{2,3},{3,2},{4,5},{5,4},{6,7},{7,6},{8,9},{9,8},{10,11... | collective-permute-start | bytes 98312 | tf_op jit(solution)/shard_map/ppermute | solution.py:402
  35.3 4.2 %collective-permute-start.17 = (bf16[4,32,128]{2,1,0:T(8,128)(2,1)S(1)}, bf16[4,32,128]{2,1,0:T(8,128)(2,1)S(1)}, u32[]{:S(2)}, u32[]{:S(2)}) collective-permute-start(bf16[4,32,128]{2,1,0:T(8,128)(2,1)S(1)} %get-tuple-element.98), channel_id=1, source_target_pairs={{0,4},{1,2},{2,1},{3,7},{4,0},{5,6},{6,5},{7,3},{8,12},{9,10},{10,... | collective-permute-start | bytes 98312 | tf_op jit(solution)/shard_map/ppermute | solution.py:402
  41.1 1.4 %collective-permute-start.19 = (bf16[12,32,128]{2,1,0:T(8,128)(2,1)S(1)}, bf16[12,32,128]{2,1,0:T(8,128)(2,1)S(1)}, u32[]{:S(2)}, u32[]{:S(2)}) collective-permute-start(bf16[12,32,128]{2,1,0:T(8,128)(2,1)S(1)} %get-tuple-element.102), channel_id=1, source_target_pairs={{0,4},{1,5},{2,6},{3,7},{4,0},{5,1},{6,2},{7,3},{8,12},{9,13},{10,... | collective-permute-start | bytes 294920 | tf_op jit(solution)/shard_map/ppermute | solution.py:402
  41.2 6.2 %collective-permute-start.18 = (bf16[12,32,128]{2,1,0:T(8,128)(2,1)S(1)}, bf16[12,32,128]{2,1,0:T(8,128)(2,1)S(1)}, u32[]{:S(2)}, u32[]{:S(2)}) collective-permute-start(bf16[12,32,128]{2,1,0:T(8,128)(2,1)S(1)} %get-tuple-element.101), channel_id=1, source_target_pairs={{0,1},{1,0},{2,3},{3,2},{4,8},{5,9},{6,10},{7,11},{8,4},{9,5},{10,... | collective-permute-start | bytes 294920 | tf_op jit(solution)/shard_map/ppermute | solution.py:402
  42.5 9.0 %collective-permute-start.20 = (bf16[16,32,128]{2,1,0:T(8,128)(2,1)S(1)}, bf16[16,32,128]{2,1,0:T(8,128)(2,1)S(1)}, u32[]{:S(2)}, u32[]{:S(2)}) collective-permute-start(bf16[16,32,128]{2,1,0:T(8,128)(2,1)S(1)} %get-tuple-element.103), channel_id=1, source_target_pairs={{0,1},{1,0},{2,3},{3,2},{4,5},{5,4},{6,7},{7,6},{8,9},{9,8},{10,11... | collective-permute-start | bytes 393224 | tf_op jit(solution)/shard_map/ppermute | solution.py:402
  42.6 8.9 %collective-permute-start.21 = (bf16[16,32,128]{2,1,0:T(8,128)(2,1)S(1)}, bf16[16,32,128]{2,1,0:T(8,128)(2,1)S(1)}, u32[]{:S(2)}, u32[]{:S(2)}) collective-permute-start(bf16[16,32,128]{2,1,0:T(8,128)(2,1)S(1)} %get-tuple-element.104), channel_id=1, source_target_pairs={{0,4},{1,2},{2,1},{3,7},{4,0},{5,6},{6,5},{7,3},{8,12},{9,10},{10,... | collective-permute-start | bytes 393224 | tf_op jit(solution)/shard_map/ppermute | solution.py:402
  47.4 4.0 %collective-permute-start.22 = (bf16[4,32,128]{2,1,0:T(8,128)(2,1)S(1)}, bf16[4,32,128]{2,1,0:T(8,128)(2,1)S(1)}, u32[]{:S(2)}, u32[]{:S(2)}) collective-permute-start(bf16[4,32,128]{2,1,0:T(8,128)(2,1)S(1)} %get-tuple-element.105), channel_id=1, source_target_pairs={{0,1},{1,0},{2,3},{3,2},{4,5},{5,4},{6,7},{7,6},{8,9},{9,8},{10,11... | collective-permute-start | bytes 98312 | tf_op jit(solution)/shard_map/ppermute | solution.py:402
  47.5 4.0 %collective-permute-start.23 = (bf16[4,32,128]{2,1,0:T(8,128)(2,1)S(1)}, bf16[4,32,128]{2,1,0:T(8,128)(2,1)S(1)}, u32[]{:S(2)}, u32[]{:S(2)}) collective-permute-start(bf16[4,32,128]{2,1,0:T(8,128)(2,1)S(1)} %get-tuple-element.106), channel_id=1, source_target_pairs={{0,4},{1,2},{2,1},{3,7},{4,0},{5,6},{6,5},{7,3},{8,12},{9,10},{10,... | collective-permute-start | bytes 98312 | tf_op jit(solution)/shard_map/ppermute | solution.py:402
  53.1 1.4 %collective-permute-start.25 = (bf16[12,32,128]{2,1,0:T(8,128)(2,1)S(1)}, bf16[12,32,128]{2,1,0:T(8,128)(2,1)S(1)}, u32[]{:S(2)}, u32[]{:S(2)}) collective-permute-start(bf16[12,32,128]{2,1,0:T(8,128)(2,1)S(1)} %get-tuple-element.110), channel_id=1, source_target_pairs={{0,4},{1,5},{2,6},{3,7},{4,0},{5,1},{6,2},{7,3},{8,12},{9,13},{10,... | collective-permute-start | bytes 294920 | tf_op jit(solution)/shard_map/ppermute | solution.py:402
  53.2 6.2 %collective-permute-start.24 = (bf16[12,32,128]{2,1,0:T(8,128)(2,1)S(1)}, bf16[12,32,128]{2,1,0:T(8,128)(2,1)S(1)}, u32[]{:S(2)}, u32[]{:S(2)}) collective-permute-start(bf16[12,32,128]{2,1,0:T(8,128)(2,1)S(1)} %get-tuple-element.109), channel_id=1, source_target_pairs={{0,1},{1,0},{2,3},{3,2},{4,8},{5,9},{6,10},{7,11},{8,4},{9,5},{10,... | collective-permute-start | bytes 294920 | tf_op jit(solution)/shard_map/ppermute | solution.py:402
  54.6 9.0 %collective-permute-start.26 = (bf16[16,32,128]{2,1,0:T(8,128)(2,1)S(1)}, bf16[16,32,128]{2,1,0:T(8,128)(2,1)S(1)}, u32[]{:S(2)}, u32[]{:S(2)}) collective-permute-start(bf16[16,32,128]{2,1,0:T(8,128)(2,1)S(1)} %get-tuple-element.111), channel_id=1, source_target_pairs={{0,1},{1,0},{2,3},{3,2},{4,5},{5,4},{6,7},{7,6},{8,9},{9,8},{10,11... | collective-permute-start | bytes 393224 | tf_op jit(solution)/shard_map/ppermute | solution.py:402
  54.7 8.9 %collective-permute-start.27 = (bf16[16,32,128]{2,1,0:T(8,128)(2,1)S(1)}, bf16[16,32,128]{2,1,0:T(8,128)(2,1)S(1)}, u32[]{:S(2)}, u32[]{:S(2)}) collective-permute-start(bf16[16,32,128]{2,1,0:T(8,128)(2,1)S(1)} %get-tuple-element.112), channel_id=1, source_target_pairs={{0,4},{1,2},{2,1},{3,7},{4,0},{5,6},{6,5},{7,3},{8,12},{9,10},{10,... | collective-permute-start | bytes 393224 | tf_op jit(solution)/shard_map/ppermute | solution.py:402
  59.5 4.0 %collective-permute-start.28 = (bf16[4,32,128]{2,1,0:T(8,128)(2,1)S(1)}, bf16[4,32,128]{2,1,0:T(8,128)(2,1)S(1)}, u32[]{:S(2)}, u32[]{:S(2)}) collective-permute-start(bf16[4,32,128]{2,1,0:T(8,128)(2,1)S(1)} %get-tuple-element.113), channel_id=1, source_target_pairs={{0,1},{1,0},{2,3},{3,2},{4,5},{5,4},{6,7},{7,6},{8,9},{9,8},{10,11... | collective-permute-start | bytes 98312 | tf_op jit(solution)/shard_map/ppermute | solution.py:402
  59.6 4.0 %collective-permute-start.29 = (bf16[4,32,128]{2,1,0:T(8,128)(2,1)S(1)}, bf16[4,32,128]{2,1,0:T(8,128)(2,1)S(1)}, u32[]{:S(2)}, u32[]{:S(2)}) collective-permute-start(bf16[4,32,128]{2,1,0:T(8,128)(2,1)S(1)} %get-tuple-element.114), channel_id=1, source_target_pairs={{0,4},{1,2},{2,1},{3,7},{4,0},{5,6},{6,5},{7,3},{8,12},{9,10},{10,... | collective-permute-start | bytes 98312 | tf_op jit(solution)/shard_map/ppermute | solution.py:402
  65.2 1.3 %collective-permute-start.31 = (bf16[6,32,128]{2,1,0:T(8,128)(2,1)S(1)}, bf16[6,32,128]{2,1,0:T(8,128)(2,1)S(1)}, u32[]{:S(2)}, u32[]{:S(2)}) collective-permute-start(bf16[6,32,128]{2,1,0:T(8,128)(2,1)S(1)} %get-tuple-element.118), channel_id=1, source_target_pairs={{0,4},{1,5},{2,6},{3,7},{4,0},{5,1},{6,2},{7,3},{8,12},{9,13},{10,... | collective-permute-start | bytes 147464 | tf_op jit(solution)/shard_map/ppermute | solution.py:402
  65.3 5.7 %collective-permute-start.30 = (bf16[6,32,128]{2,1,0:T(8,128)(2,1)S(1)}, bf16[6,32,128]{2,1,0:T(8,128)(2,1)S(1)}, u32[]{:S(2)}, u32[]{:S(2)}) collective-permute-start(bf16[6,32,128]{2,1,0:T(8,128)(2,1)S(1)} %get-tuple-element.117), channel_id=1, source_target_pairs={{0,1},{1,0},{2,3},{3,2},{4,8},{5,9},{6,10},{7,11},{8,4},{9,5},{10,... | collective-permute-start | bytes 147464 | tf_op jit(solution)/shard_map/ppermute | solution.py:402
  66.5 8.3 %collective-permute-start.32 = (bf16[7,32,128]{2,1,0:T(8,128)(2,1)S(1)}, bf16[7,32,128]{2,1,0:T(8,128)(2,1)S(1)}, u32[]{:S(2)}, u32[]{:S(2)}) collective-permute-start(bf16[7,32,128]{2,1,0:T(8,128)(2,1)S(1)} %get-tuple-element.119), channel_id=1, source_target_pairs={{0,1},{1,0},{2,3},{3,2},{4,5},{5,4},{6,7},{7,6},{8,9},{9,8},{10,11... | collective-permute-start | bytes 172040 | tf_op jit(solution)/shard_map/ppermute | solution.py:402
  66.6 8.2 %collective-permute-start.33 = (bf16[7,32,128]{2,1,0:T(8,128)(2,1)S(1)}, bf16[7,32,128]{2,1,0:T(8,128)(2,1)S(1)}, u32[]{:S(2)}, u32[]{:S(2)}) collective-permute-start(bf16[7,32,128]{2,1,0:T(8,128)(2,1)S(1)} %get-tuple-element.120), channel_id=1, source_target_pairs={{0,4},{1,2},{2,1},{3,7},{4,0},{5,6},{6,5},{7,3},{8,12},{9,10},{10,... | collective-permute-start | bytes 172040 | tf_op jit(solution)/shard_map/ppermute | solution.py:402
  71.0 3.7 %collective-permute-start.34 = (bf16[1,32,128]{2,1,0:T(8,128)(2,1)S(1)}, bf16[1,32,128]{2,1,0:T(8,128)(2,1)S(1)}, u32[]{:S(2)}, u32[]{:S(2)}) collective-permute-start(bf16[1,32,128]{2,1,0:T(8,128)(2,1)S(1)} %get-tuple-element.121), channel_id=1, source_target_pairs={{0,1},{1,0},{2,3},{3,2},{4,5},{5,4},{6,7},{7,6},{8,9},{9,8},{10,11... | collective-permute-start | bytes 24584 | tf_op jit(solution)/shard_map/ppermute | solution.py:402
  71.1 3.7 %collective-permute-start.35 = (bf16[1,32,128]{2,1,0:T(8,128)(2,1)S(1)}, bf16[1,32,128]{2,1,0:T(8,128)(2,1)S(1)}, u32[]{:S(2)}, u32[]{:S(2)}) collective-permute-start(bf16[1,32,128]{2,1,0:T(8,128)(2,1)S(1)} %get-tuple-element.122), channel_id=1, source_target_pairs={{0,4},{1,2},{2,1},{3,7},{4,0},{5,6},{6,5},{7,3},{8,12},{9,10},{10,... | collective-permute-start | bytes 24584 | tf_op jit(solution)/shard_map/ppermute | solution.py:402
